TPU v7x, 256 devices: a whole 4x4x8 slice. The times are simulated.
256 devices in a mesh: row: 8 (over y_lo, x), col: 32 (over y_hi, z, core).
Axes of the slice: x: 4, y: 4 (y_hi: 2, y_lo: 2; y = y_hi * 2 + y_lo), z: 8, core: 2. Of those that a mesh axis runs over, the one named last changes fastest.
Arguments:
- tokens: float32 [128, 512, 256], P('row', 'col'), may hold values from -6 to 6
- region_ids: int32 [128, 512], P('row', 'col'), may hold values from 0 to 15, as said below
- bias_index: int32 [256, 256], replicated, may hold values from 0 to 960
- norm_gain: float32 [2, 2, 256], replicated, may hold values from 0.1 to 1.9
- norm_shift: float32 [2, 2, 256], replicated, may hold values from -3 to 3
- qkv_weight: bfloat16 [2, 256, 768], replicated
- proj_weight: bfloat16 [2, 256, 256], replicated, may hold values from -0.375 to 0.375
- expand_weight: bfloat16 [2, 256, 1024], replicated, may hold values from -0.375 to 0.375
- reduce_weight: bfloat16 [2, 1024, 256], replicated, may hold values from -0.1875 to 0.1875
- bias_table: float32 [2, 8, 961], replicated, may hold values from -4 to 4
Outputs:
- mixed_map: float32 [128, 512, 256], P('row', 'col')
Inputs may be any that keep to these rules, and one draw needn't show every extreme that they name: `region_ids`: the map is cut into rectangles by three row cuts and three column cuts; a position's label is 4 times its row band plus its column band.
All inputs are finite; a program needn't handle non-finite values.
Results may differ from a plain program's by a relative error of at most 0.019.
Values sent between devices are 32-bit elements; how exact they have to be, the bound alone decides.
No kernel may reach another device: no remote copies, remote signals or barrier semaphores. Data moves between devices by JAX's collectives and lax.ppermute only.
A program may use at most 128 MiB of HBM per device.

v0:
```python
import jax
import jax.numpy as jnp
from jax import lax
from jax.sharding import PartitionSpec as P

HEADS = 8
WIN = 16
SHIFT = 8


def from_behind(x, axis, by):
    peers = lax.axis_size(axis)
    return lax.ppermute(x, axis, [(i, (i + by) % peers) for i in range(peers)])


def layer_norm(tile, gain, offset):
    center = tile - jnp.mean(tile, -1, keepdims=True)
    spread = jnp.mean(center * center, -1, keepdims=True)
    return (center * lax.rsqrt(spread + 1e-05) * gain + offset).astype(jnp.bfloat16)


def to_windows(array, tile_rows, tile_cols):
    array = array.reshape(tile_rows // WIN, WIN, tile_cols // WIN, WIN)
    return jnp.transpose(array, (0, 2, 1, 3)).reshape(-1, WIN * WIN)


def swin_block(
    tile,
    layer,
    region,
    bias_index,
    norm_gain,
    norm_shift,
    qkv_weight,
    proj_weight,
    expand_weight,
    reduce_weight,
    bias_table,
):
    tile_rows, tile_cols, channels = tile.shape
    head_count = HEADS
    head_size = channels // head_count
    win_rows = tile_rows // WIN
    win_cols = tile_cols // WIN
    normed = layer_norm(tile, norm_gain[layer, 0], norm_shift[layer, 0])
    flat = normed.reshape(-1, channels)
    projected = lax.dot_general(
        qkv_weight[layer], flat, (((0,), (1,)), ((), ())), preferred_element_type=jnp.float32
    ).astype(jnp.bfloat16)
    projected = projected.reshape(3, head_count, head_size, win_rows, WIN, win_cols, WIN)
    projected = jnp.transpose(projected, (0, 3, 5, 1, 2, 4, 6)).reshape(
        3, win_rows * win_cols, head_count, head_size, WIN * WIN
    )
    query = projected[0]
    keys = projected[1]
    values = projected[2]
    bias = bias_table[layer][:, bias_index]
    scores = (
        jnp.einsum("nhdq,nhdk->nhqk", query, keys, preferred_element_type=jnp.float32)
        * head_size ** (-0.5)
        + bias[None]
    )
    if region is not None:
        window_region = to_windows(region, tile_rows, tile_cols)
        same_region = window_region[:, :, None] == window_region[:, None, :]
        scores = jnp.where(same_region[:, None], scores, -jnp.inf)
    row_max = jnp.max(scores, -1, keepdims=True)
    raw_weights = jnp.exp(scores - row_max)
    weights = (raw_weights / jnp.sum(raw_weights, -1, keepdims=True)).astype(jnp.bfloat16)
    mixed = jnp.einsum(
        "nhqk,nhdk->nhdq", weights, values, preferred_element_type=jnp.float32
    ).astype(jnp.bfloat16)
    mixed = mixed.reshape(win_rows, win_cols, channels, WIN, WIN)
    mixed = jnp.transpose(mixed, (0, 3, 1, 4, 2)).reshape(-1, channels)
    attended = tile + jnp.dot(
        mixed, proj_weight[layer], preferred_element_type=jnp.float32
    ).reshape(tile_rows, tile_cols, channels)
    normed_two = layer_norm(attended, norm_gain[layer, 1], norm_shift[layer, 1])
    hidden = jax.nn.gelu(
        jnp.dot(
            normed_two.reshape(-1, channels),
            expand_weight[layer],
            preferred_element_type=jnp.float32,
        ),
        approximate=False,
    ).astype(jnp.bfloat16)
    return attended + jnp.dot(
        hidden, reduce_weight[layer], preferred_element_type=jnp.float32
    ).reshape(tile_rows, tile_cols, channels)


def move_columns(tile, forward):
    if forward:
        edge = tile[:, :SHIFT]
        step_dir = -1
    else:
        edge = tile[:, -SHIFT:]
        step_dir = 1
    moved = from_behind(edge, "col", step_dir)
    if forward:
        return jnp.concatenate([tile[:, SHIFT:], moved], 1)
    return jnp.concatenate([moved, tile[:, :-SHIFT]], 1)


def move_rows(tile, forward):
    if forward:
        edge = tile[:SHIFT]
        step_dir = -1
    else:
        edge = tile[-SHIFT:]
        step_dir = 1
    moved = from_behind(edge, "row", step_dir)
    if forward:
        return jnp.concatenate([tile[SHIFT:], moved], 0)
    return jnp.concatenate([moved, tile[:-SHIFT]], 0)


def roll_tile(tile, forward):
    return move_rows(move_columns(tile, forward), forward)


def per_device(
    tokens,
    region_ids,
    bias_index,
    norm_gain,
    norm_shift,
    qkv_weight,
    proj_weight,
    expand_weight,
    reduce_weight,
    bias_table,
):
    weights_all = (
        bias_index,
        norm_gain,
        norm_shift,
        qkv_weight,
        proj_weight,
        expand_weight,
        reduce_weight,
        bias_table,
    )
    first = swin_block(tokens, 0, None, *weights_all)
    rolled = roll_tile(first, True)
    second = swin_block(rolled, 1, region_ids, *weights_all)
    return roll_tile(second, False)


def solution(mesh):
    in_specs = (P("row", "col", None), P("row", "col"), P(), P(), P(), P(), P(), P(), P(), P())
    out_specs = P("row", "col", None)
    return jax.shard_map(
        per_device, mesh=mesh, in_specs=in_specs, out_specs=out_specs, check_vma=False
    )
```

profile of v0, /device:TPU:8, one launch (start us, length us, event | category | flops | bytes accessed | tf_op | source)
XLA Modules:
  0.0 536.0 jit_solution(6789101406535367946)
XLA Ops:
  0.8 1.3 fusion.62
  2.1 1.1 reduce_sum.90
  3.1 1.1 multiply_reduce_fusion.3
  4.3 1.1 add_convert_fusion.3
  5.4 1.3 fusion.3
  8.0 215.5 %gather_fusion = f32[65536,8]{1,0:T(8,128)} fusion(f32[8,961]{0,1:T(8,128)S(1)} %bitcast.108, s32[65536]{0:T(1024)S(1)} %broadcast_clamp_fusion), kind=kCustom, calls=%fused_computation | custom fusion | bytes 4456448 | tf_op jit(solution)/shard_map/gather | solution.py:57
  223.5 18.7 %copy.28 = f32[256,256,8]{0,1,2:T(8,128)S(1)} copy(f32[256,256,8]{2,1,0:T(8,128)} %bitcast.110) | data formatting | bytes 4194304 | tf_op jit(solution)/shard_map/gather | solution.py:57
  242.7 1.3 copy-done.1
  244.6 2.8 convolution_convert_fusion.3
  248.8 3.5 fusion.7
  253.3 7.0 %collective-permute-start = (f32[16,8,256]{2,1,0:T(8,128)}, f32[16,8,256]{2,1,0:T(8,128)}, u32[]{:S(2)}, u32[]{:S(2)}) collective-permute-start(f32[16,8,256]{2,1,0:T(8,128)} %get-tuple-element.16), channel_id=1, source_target_pairs={{0,31},{1,0},{2,1},{3,2},{4,3},{5,4},{6,5},{7,6},{8,7},{9,8},{10,9... | collective-permute-start | bytes 393224 | tf_op jit(solution)/shard_map/ppermute | solution.py:13
  260.6 215.5 %gather_fusion.1 = f32[65536,8]{1,0:T(8,128)} fusion(f32[8,961]{0,1:T(8,128)S(1)} %bitcast.107, s32[65536]{0:T(1024)S(1)} %broadcast_clamp_fusion), kind=kCustom, calls=%fused_computation.1 | custom fusion | bytes 4456448 | tf_op jit(solution)/shard_map/gather | solution.py:57
  476.1 18.7 %copy.36 = f32[256,256,8]{0,1,2:T(8,128)S(1)} copy(f32[256,256,8]{2,1,0:T(8,128)} %bitcast.109) | data formatting | bytes 4194304 | tf_op jit(solution)/shard_map/gather | solution.py:57
  495.8 3.8 collective-permute-start.1
  500.3 1.8 collective-permute-done.1
  503.2 1.3 fusion.4
  505.2 1.0 copy.32
  506.2 1.6 copy.33
  507.9 1.4 fusion.2
  509.3 1.3 copy-done
  511.7 2.8 convolution_convert_fusion.2
  515.8 2.6 fusion.10
  518.9 9.2 %collective-permute-done.2 = f32[16,8,256]{2,1,0:T(8,128)S(1)} collective-permute-done((f32[16,8,256]{2,1,0:T(8,128)S(1)}, f32[16,8,256]{2,1,0:T(8,128)S(1)}, u32[]{:S(2)}, u32[]{:S(2)}) %collective-permute-start.2) | collective-permute-done | bytes 131104 | tf_op jit(solution)/shard_map/ppermute | solution.py:13
  528.2 7.1 %collective-permute-done.3 = f32[8,16,256]{2,1,0:T(8,128)S(1)} collective-permute-done((f32[8,16,256]{2,1,0:T(8,128)S(1)}, f32[8,16,256]{2,1,0:T(8,128)S(1)}, u32[]{:S(2)}, u32[]{:S(2)}) %collective-permute-start.3) | collective-permute-done | bytes 131104 | tf_op jit(solution)/shard_map/ppermute | solution.py:13
  (71 shorter events, 12.5 us)
Async XLA Ops:
  0.0 7.0 %copy-start.7 = (s32[256,256]{1,0:T(8,128)S(1)}, s32[256,256]{1,0:T(8,128)}, u32[]{:S(2)}) copy-start(s32[256,256]{1,0:T(8,128)} %param.12) | copy-start | bytes 786436
  4.3 2.9 copy-start.9
  242.7 1.4 copy-start.1
  244.6 3.5 copy-start.2
  244.6 3.5 copy-start.5
  248.8 3.6 copy-start.3
  252.3 8.0 %copy-start.8 = (f32[1,8,961]{2,1,0:T(8,128)S(1)}, f32[1,8,961]{2,1,0:T(8,128)}, u32[]{:S(2)}) copy-start(f32[1,8,961]{2,1,0:T(8,128)} %get-tuple-element.17) | copy-start | bytes 92260
  253.3 241.5 %collective-permute-start = (f32[16,8,256]{2,1,0:T(8,128)}, f32[16,8,256]{2,1,0:T(8,128)}, u32[]{:S(2)}, u32[]{:S(2)}) collective-permute-start(f32[16,8,256]{2,1,0:T(8,128)} %get-tuple-element.16), channel_id=1, source_target_pairs={{0,31},{1,0},{2,1},{3,2},{4,3},{5,4},{6,5},{7,6},{8,7},{9,8},{10,9... | collective-permute-start | bytes 393224 | tf_op jit(solution)/shard_map/ppermute | solution.py:13
  476.1 18.7 %copy-start.10 = (s32[16,16]{1,0:T(8,128)S(1)}, s32[16,16]{1,0:T(8,128)}, u32[]{:S(2)}) copy-start(s32[16,16]{1,0:T(8,128)} %param.11) | copy-start | bytes 3076
  495.8 6.3 %collective-permute-start.1 = (f32[8,16,256]{2,1,0:T(8,128)S(1)}, f32[8,16,256]{2,1,0:T(8,128)S(1)}, u32[]{:S(2)}, u32[]{:S(2)}) collective-permute-start(f32[8,16,256]{2,1,0:T(8,128)S(1)} %get-tuple-element.14), channel_id=1, source_target_pairs={{0,224},{32,0},{64,32},{96,64},{128,96},{160,128},{192,160},{224,1... | collective-permute-start | bytes 393224 | tf_op jit(solution)/shard_map/ppermute | solution.py:13
  509.3 1.4 copy-start
  510.6 0.9 copy-start.4
  511.7 3.5 copy-start.6
  514.5 1.3 copy-start.11
  518.8 9.3 %collective-permute-start.2 = (f32[16,8,256]{2,1,0:T(8,128)S(1)}, f32[16,8,256]{2,1,0:T(8,128)S(1)}, u32[]{:S(2)}, u32[]{:S(2)}) collective-permute-start(f32[16,8,256]{2,1,0:T(8,128)S(1)} %get-tuple-element.11), channel_id=1, source_target_pairs={{0,1},{1,2},{2,3},{3,4},{4,5},{5,6},{6,7},{7,8},{8,9},{9,10},{10,1... | collective-permute-start | bytes 393224 | tf_op jit(solution)/shard_map/ppermute | solution.py:13
  528.1 7.2 %collective-permute-start.3 = (f32[8,16,256]{2,1,0:T(8,128)S(1)}, f32[8,16,256]{2,1,0:T(8,128)S(1)}, u32[]{:S(2)}, u32[]{:S(2)}) collective-permute-start(f32[8,16,256]{2,1,0:T(8,128)S(1)} %fusion.45), channel_id=1, source_target_pairs={{0,32},{32,64},{64,96},{96,128},{128,160},{160,192},{192,224},{224... | collective-permute-start | bytes 393224 | tf_op jit(solution)/shard_map/ppermute | solution.py:13
where the time goes:
time: 537 us; the launch traced here: 536 us
  local copies, waits for them, and re-layouts  481 us (90%)
  waiting for transfers between devices  18.1 us (3%)
  matrix products  17.3 us (3%)
  starting transfers between devices  11 us (2%)
  other arithmetic  8.29 us (2%)
    gather x4, local copies, waits for them, and re-layouts, swin_block(): bias = bias_table[layer][:, bias_index]  468 us
    ppermute x4, waiting for transfers between devices, from_behind(): return lax.ppermute(x, axis, [(i, (i + by) % peers) for i in range(peers)])  18.1 us
    ppermute x4, starting transfers between devices, from_behind(): return lax.ppermute(x, axis, [(i, (i + by) % peers) for i in range(peers)])  11 us
  transfers between devices with their start and end apart: 4, of which 3 were waited for; matrix products, arithmetic and copies ran while one was open for 44% of the time, Pallas kernels for 0%

commit v1 on v0

v1 whole, which is shorter than its diff:
```python
import functools
import math

import jax
import jax.numpy as jnp
from jax import lax
from jax.experimental import pallas as pl
from jax.experimental.pallas import tpu as pltpu
from jax.sharding import PartitionSpec as P

HEADS = 8
LOG2E = math.log2(math.e)
ENTRIES = 961
FIXED = 8000.0
F32 = jnp.float32
BF16 = jnp.bfloat16


def take_lanes(x, lanes):
    return jnp.take_along_axis(x, lanes, axis=1, mode="promise_in_bounds")


def fill_lookup(table, lookup_ref):
    table = jnp.concatenate([table, jnp.zeros((HEADS, 1024 - ENTRIES), F32)], 1)
    fixed = jnp.round(table * FIXED).astype(jnp.int32)
    for pair in range(HEADS // 2):
        packed = (fixed[2 * pair : 2 * pair + 1] << 16) + fixed[2 * pair + 1 : 2 * pair + 2]
        for chunk in range(8):
            lookup_ref[pair * 8 + chunk] = jnp.broadcast_to(
                packed[:, chunk * 128 : chunk * 128 + 128], (8, 128)
            )


def look_up_bias(lookup_ref, index_ref, bias_ref, rows=4, same=None):
    scale = LOG2E / FIXED / 65536

    def tile(row):
        for half in range(2):
            lanes = slice(half * 128, half * 128 + 128)
            index = index_ref[pl.ds(row, 8), lanes]
            low = index & 127
            bits = [(index & bit) != 0 for bit in (128, 256, 512)]
            keep = None if same is None else same(row, lanes)
            for pair in range(HEADS // 2):
                found = [take_lanes(lookup_ref[pair * 8 + chunk], low) for chunk in range(8)]
                for bit in bits:
                    found = [
                        jnp.where(bit, found[2 * i + 1], found[2 * i])
                        for i in range(len(found) // 2)
                    ]
                first = found[0].astype(F32) * scale
                second = (found[0] << 16).astype(F32) * scale
                if keep is not None:
                    first = jnp.where(keep, first, -jnp.inf)
                    second = jnp.where(keep, second, -jnp.inf)
                bias_ref[2 * pair, pl.ds(row, 8), lanes] = first
                bias_ref[2 * pair + 1, pl.ds(row, 8), lanes] = second

    def step(i, carry):
        for sub in range(rows):
            tile(pl.multiple_of(i * (8 * rows) + sub * 8, 8))
        return carry

    lax.fori_loop(0, 32 // rows, step, 0)


def layer_norm(x, gain, shift):
    center = x - jnp.mean(x, -1, keepdims=True)
    spread = jnp.mean(center * center, -1, keepdims=True)
    return (center * lax.rsqrt(spread + 1e-05) * gain + shift).astype(BF16)


def attention(x, normed, bias_ref, wqkv, wproj, joined_ref):
    query = jnp.dot(normed, wqkv[:, 0:256], preferred_element_type=F32)
    query = (query * (LOG2E / math.sqrt(32.0))).astype(BF16)
    keys = jnp.dot(normed, wqkv[:, 256:512], preferred_element_type=F32).astype(BF16)
    values = jnp.dot(normed, wqkv[:, 512:768], preferred_element_type=F32).T.astype(BF16)
    ones = jnp.ones((16, 256), BF16)
    head_of_lane = lax.broadcasted_iota(jnp.int32, (1, 128), 1) // 32
    for h in range(HEADS):
        group = slice((h // 4) * 128, (h // 4) * 128 + 128)
        own = jnp.where(head_of_lane == h % 4, 1.0, 0.0).astype(BF16)
        scores = lax.dot_general(
            keys[:, group], query[:, group] * own, (((1,), (1,)), ((), ())), preferred_element_type=F32
        )
        scores = scores + bias_ref[h]
        raw = jnp.exp2(scores - jnp.max(scores, 0, keepdims=True)).astype(BF16)
        left = jnp.concatenate([values[32 * h : 32 * h + 32], ones], 0)
        out = jnp.dot(left, raw, preferred_element_type=F32)
        inverse = 1.0 / out[32:40]
        for j in range(2):
            part = jnp.concatenate(
                [out[16 * j : 16 * j + 8] * inverse, out[16 * j + 8 : 16 * j + 16] * inverse], 0
            )
            joined_ref[32 * h + 16 * j : 32 * h + 16 * j + 16, :] = part.astype(BF16)
    return x + lax.dot_general(
        joined_ref[...], wproj[...], (((0,), (0,)), ((), ())), preferred_element_type=F32
    )


def feed_forward(attended, normed, wexpand, wreduce):
    total = attended
    for j in range(4):
        part = slice(j * 256, j * 256 + 256)
        hidden = jnp.dot(normed, wexpand[:, part], preferred_element_type=F32)
        hidden = (hidden * (0.5 * lax.erf(hidden * math.sqrt(0.5)) + 0.5)).astype(BF16)
        total = total + jnp.dot(hidden, wreduce[part, :], preferred_element_type=F32)
    return total


def write_quadrants(total, outs):
    cells = total.reshape(2, 8, 2, 8, 256)
    for a in range(2):
        for b in range(2):
            outs[2 * a + b][...] = cells[a, :, b]


def first_kernel(
    x_hbm, index_hbm, table_hbm, gain_hbm, shift_hbm, wqkv_hbm, wproj_hbm, wexpand_hbm, wreduce_hbm,
    out00, out01, out10, out11,
    x, index, table, gain, shift, wqkv, wproj, wexpand, wreduce, lookup, index_t, bias, joined, sems,
):
    moves = [
        (index_hbm, index), (table_hbm.at[0], table), (x_hbm, x), (gain_hbm.at[0], gain), (shift_hbm.at[0], shift),
        (wqkv_hbm.at[0], wqkv), (wproj_hbm.at[0], wproj), (wexpand_hbm.at[0], wexpand), (wreduce_hbm.at[0], wreduce),
    ]
    copies = [pltpu.make_async_copy(src, dst, sems.at[i]) for i, (src, dst) in enumerate(moves)]
    for copy in copies:
        copy.start()
    copies[0].wait()
    copies[1].wait()
    index_t[...] = index[...].T
    fill_lookup(table[...], lookup)
    look_up_bias(lookup, index_t, bias)
    for copy in copies[2:7]:
        copy.wait()
    tile = x[...].reshape(256, 256)
    normed = layer_norm(tile, gain[0:1], shift[0:1])
    attended = attention(tile, normed, bias, wqkv, wproj, joined)
    copies[7].wait()
    copies[8].wait()
    normed = layer_norm(attended, gain[1:2], shift[1:2])
    write_quadrants(feed_forward(attended, normed, wexpand, wreduce), (out00, out01, out10, out11))


def bias_kernel(index, table, region, bias, lookup, index_t, row_label, col_label):
    index_t[...] = index[...].T
    fill_lookup(table[1], lookup)
    labels = region[...].astype(F32).astype(BF16)
    tall_at = lax.broadcasted_iota(jnp.int32, (256, 16), 0)
    tall_lane = lax.broadcasted_iota(jnp.int32, (256, 16), 1)
    wide_at = lax.broadcasted_iota(jnp.int32, (16, 256), 1)
    wide_row = lax.broadcasted_iota(jnp.int32, (16, 256), 0)
    pick_row = jnp.where(tall_at // 16 == tall_lane, 1.0, 0.0).astype(BF16)
    pick_col = jnp.where(wide_at % 16 == wide_row, 1.0, 0.0).astype(BF16)
    tall = jnp.dot(pick_row, labels, preferred_element_type=F32)
    tall = jnp.sum(jnp.where(tall_at % 16 == tall_lane, tall, 0.0), 1, keepdims=True)
    wide = jnp.dot(labels, pick_col, preferred_element_type=F32)
    wide = jnp.sum(jnp.where(wide_at // 16 == wide_row, wide, 0.0), 0, keepdims=True)
    col_label[...] = jnp.broadcast_to(tall, (256, 128))
    row_label[...] = jnp.broadcast_to(wide, (8, 256))

    def same(row, lanes):
        return col_label[pl.ds(row, 8), :] == row_label[:, lanes]

    look_up_bias(lookup, index_t, bias, same=same)


def second_kernel(
    in00, in01, in10, in11, bias, gain, shift, wqkv, wproj, wexpand, wreduce,
    out00, out01, out10, out11, joined,
):
    top = jnp.stack([in00[...], in01[...]], 1)
    bottom = jnp.stack([in10[...], in11[...]], 1)
    tile = jnp.concatenate([top, bottom], 0).reshape(256, 256)
    normed = layer_norm(tile, gain[1, 0:1], shift[1, 0:1])
    attended = attention(tile, normed, bias, wqkv.at[1], wproj.at[1], joined)
    normed = layer_norm(attended, gain[1, 1:2], shift[1, 1:2])
    total = feed_forward(attended, normed, wexpand.at[1], wreduce.at[1])
    write_quadrants(total, (out00, out01, out10, out11))


def shifted(x, rows, cols, by_row, by_col):
    if by_row == 0:
        return lax.ppermute(x, "col", [((c + by_col) % cols, c) for c in range(cols)])
    if by_col == 0:
        return lax.ppermute(x, "row", [((r + by_row) % rows, r) for r in range(rows)])
    pairs = [
        ((r + by_row) % rows * cols + (c + by_col) % cols, r * cols + c)
        for r in range(rows)
        for c in range(cols)
    ]
    return lax.ppermute(x, ("row", "col"), pairs)


def per_device(rows, cols, tokens, region, index, gain, shift, wqkv, wproj, wexpand, wreduce, table):
    hbm = pl.BlockSpec(memory_space=pltpu.HBM)
    vmem = pl.BlockSpec(memory_space=pltpu.VMEM)
    quadrant = jax.ShapeDtypeStruct((8, 8, 256), F32)
    q00, q01, q10, q11 = pl.pallas_call(
        first_kernel,
        out_shape=[quadrant] * 4,
        in_specs=[hbm] * 9,
        out_specs=[vmem] * 4,
        scratch_shapes=[
            pltpu.VMEM((16, 16, 256), F32),
            pltpu.VMEM((256, 256), jnp.int32),
            pltpu.VMEM((HEADS, ENTRIES), F32),
            pltpu.VMEM((2, 256), F32),
            pltpu.VMEM((2, 256), F32),
            pltpu.VMEM((256, 768), BF16),
            pltpu.VMEM((256, 256), BF16),
            pltpu.VMEM((256, 1024), BF16),
            pltpu.VMEM((1024, 256), BF16),
            pltpu.VMEM((32, 8, 128), jnp.int32),
            pltpu.VMEM((256, 256), jnp.int32),
            pltpu.VMEM((HEADS, 256, 256), F32),
            pltpu.VMEM((256, 256), BF16),
            pltpu.SemaphoreType.DMA((9,)),
        ],
        compiler_params=pltpu.CompilerParams(vmem_limit_bytes=63 << 20),
        cost_estimate=pl.CostEstimate(flops=10**9, bytes_accessed=3 << 20, transcendentals=0),
    )(tokens, index, table, gain, shift, wqkv, wproj, wexpand, wreduce)
    r01 = shifted(q10, rows, cols, 0, 1)
    r10 = shifted(q01, rows, cols, 1, 0)
    r11 = shifted(q00, rows, cols, 1, 1)
    bias = pl.pallas_call(
        bias_kernel,
        out_shape=jax.ShapeDtypeStruct((HEADS, 256, 256), F32),
        in_specs=[vmem] * 3,
        out_specs=vmem,
        scratch_shapes=[
            pltpu.VMEM((32, 8, 128), jnp.int32),
            pltpu.VMEM((256, 256), jnp.int32),
            pltpu.VMEM((8, 256), F32),
            pltpu.VMEM((256, 128), F32),
        ],
        compiler_params=pltpu.CompilerParams(vmem_limit_bytes=16 << 20),
        cost_estimate=pl.CostEstimate(flops=10**9, bytes_accessed=8 << 20, transcendentals=0),
    )(index, table, region)
    s00, s01, s10, s11 = pl.pallas_call(
        second_kernel,
        out_shape=[quadrant] * 4,
        in_specs=[vmem] * 11,
        out_specs=[vmem] * 4,
        scratch_shapes=[pltpu.VMEM((256, 256), BF16)],
        compiler_params=pltpu.CompilerParams(vmem_limit_bytes=16 << 20),
        cost_estimate=pl.CostEstimate(flops=10**9, bytes_accessed=3 << 20, transcendentals=0),
    )(q11, r01, r10, r11, bias, gain, shift, wqkv, wproj, wexpand, wreduce)
    t10 = shifted(s01, rows, cols, 0, -1)
    t01 = shifted(s10, rows, cols, -1, 0)
    t00 = shifted(s11, rows, cols, -1, -1)
    top = jnp.concatenate([t00, t01], 1)
    bottom = jnp.concatenate([t10, s00], 1)
    return jnp.concatenate([top, bottom], 0)


def solution(mesh):
    in_specs = (P("row", "col", None), P("row", "col"), P(), P(), P(), P(), P(), P(), P(), P())
    body = functools.partial(per_device, mesh.shape["row"], mesh.shape["col"])
    return jax.shard_map(
        body, mesh=mesh, in_specs=in_specs, out_specs=P("row", "col", None), check_vma=False
    )
```

time: 537 us -> 37.2 us (0.07)
  the two profiles are of different devices: /device:TPU:8 before, /device:TPU:4 now
where the time goes in v1:
time: 37.2 us
  Pallas kernels  14.9 us (40%)
  starting transfers between devices  13 us (35%)
  waiting for transfers between devices  8.31 us (22%)
  other arithmetic  0.72 us (2%)
    pallas_call x1, Pallas kernels, per_device(): pl.pallas_call(first_kernel, out_shape=[quadrant] * 4, in_specs=[hbm] * 9...  8.31 us
    ppermute x2, starting transfers between devices, shifted(): lax.ppermute(x, 'col', [((c + by_col) % cols, c) for c in range(cols)])  8.01 us
    ppermute x2, waiting for transfers between devices, shifted(): return lax.ppermute(x, ('row', 'col'), pairs)  4.19 us
    ppermute x2, starting transfers between devices, shifted(): lax.ppermute(x, 'row', [((r + by_row) % rows, r) for r in range(rows)])  4.14 us
    pallas_call x1, Pallas kernels, per_device(): pl.pallas_call(second_kernel, out_shape=[quadrant] * 4, in_specs=[vmem] *...  3.41 us
    pallas_call x1, Pallas kernels, per_device(): pl.pallas_call(bias_kernel, out_shape=jax.ShapeDtypeStruct((HEADS, 256, 2...  3.21 us
    ppermute x2, waiting for transfers between devices, shifted(): lax.ppermute(x, 'col', [((c + by_col) % cols, c) for c in range(cols)])  3.11 us
    ppermute x2, waiting for transfers between devices, shifted(): lax.ppermute(x, 'row', [((r + by_row) % rows, r) for r in range(rows)])  1 us
  transfers between devices with their start and end apart: 6, of which 3 were waited for; matrix products, arithmetic and copies ran while one was open for 0% of the time, Pallas kernels for 9%

profile of v1, /device:TPU:4, one launch (start us, length us, event | category | flops | bytes accessed | tf_op | source)
XLA Modules:
  0.0 37.2 jit_solution(2451125817258107542)
XLA Ops:
  0.0 8.3 %shard_map.100 = (f32[8,8,256]{2,1,0:T(8,128)}, f32[8,8,256]{2,1,0:T(8,128)}, f32[8,8,256]{2,1,0:T(8,128)}, f32[8,8,256]{2,1,0:T(8,128)}) custom-call(f32[16,16,256]{2,1,0:T(8,128)} %x_hbm.1, s32[256,256]{1,0:T(8,128)} %index.1, f32[2,8,961]{2,1,0:T(8,128)} %table.1, f32[2,2,256]{2,1,0:T(2,128)} %gain.1, f32[2,2,256]{2,1,0:T(2,128)} %shift.1, ...), custom_call_target="tpu_custom_call" | custom-call | flops 1000000000 | bytes 3145728 | tf_op jit(solution)/shard_map/pallas_call | solution.py:200
  8.3 0.0 copy-start
  8.3 0.0 copy-start.1
  8.4 0.0 copy-start.2
  8.4 0.0 copy-start.3
  8.4 0.0 copy-start.6
  8.4 0.0 copy-start.7
  8.4 0.0 copy-start.8
  8.4 8.0 %collective-permute-start = (f32[8,8,256]{2,1,0:T(8,128)}, f32[8,8,256]{2,1,0:T(8,128)S(1)}, u32[]{:S(2)}, u32[]{:S(2)}) collective-permute-start(f32[8,8,256]{2,1,0:T(8,128)} %get-tuple-element.14), channel_id=1, source_target_pairs={{1,0},{2,1},{3,2},{4,3},{5,4},{6,5},{7,6},{8,7},{9,8},{10,9},{11,1... | collective-permute-start | bytes 196616 | tf_op jit(solution)/shard_map/ppermute | solution.py:185
  16.4 0.5 %collective-permute-start.1 = (f32[8,8,256]{2,1,0:T(8,128)}, f32[8,8,256]{2,1,0:T(8,128)S(1)}, u32[]{:S(2)}, u32[]{:S(2)}) collective-permute-start(f32[8,8,256]{2,1,0:T(8,128)} %get-tuple-element.15), channel_id=1, source_target_pairs={{32,0},{64,32},{96,64},{128,96},{160,128},{192,160},{224,192},{0,2... | collective-permute-start | bytes 196616 | tf_op jit(solution)/shard_map/ppermute | solution.py:187
  17.0 0.4 collective-permute-start.2
  17.3 3.2 %shard_map.101.bias = f32[8,256,256]{2,1,0:T(8,128)S(1)} custom-call(s32[256,256]{1,0:T(8,128)S(1)} %copy-done.4, f32[2,8,961]{2,1,0:T(8,128)S(1)} %copy-done.5, s32[16,16]{1,0:T(8,128)S(1)} %copy-done.9), custom_call_target="tpu_custom_call" | custom-call | flops 1000000000 | bytes 8388608 | tf_op jit(solution)/shard_map/pallas_call | solution.py:227
  20.5 0.0 collective-permute-done.in01
  20.6 1.0 %collective-permute-done.1.in10 = f32[8,8,256]{2,1,0:T(8,128)S(1)} collective-permute-done((f32[8,8,256]{2,1,0:T(8,128)}, f32[8,8,256]{2,1,0:T(8,128)S(1)}, u32[]{:S(2)}, u32[]{:S(2)}) %collective-permute-start.1) | collective-permute-done | bytes 65568 | tf_op jit(solution)/shard_map/ppermute | solution.py:187
  21.6 0.0 collective-permute-done.2.in11
  21.6 0.0 copy-done
  21.6 3.4 %shard_map.102 = (f32[8,8,256]{2,1,0:T(8,128)S(1)}, f32[8,8,256]{2,1,0:T(8,128)S(1)}, f32[8,8,256]{2,1,0:T(8,128)S(1)}, f32[8,8,256]{2,1,0:T(8,128)S(1)}) custom-call(f32[8,8,256]{2,1,0:T(8,128)S(1)} %copy-done.6, f32[8,8,256]{2,1,0:T(8,128)S(1)} %collective-permute-done.in01, f32[8,8,256]{2,1,0:T(8,128)S(1)} %collective-permute-done.1.in10, ...), custom_call_target="tpu_custom_call" | custom-call | flops 1000000000 | bytes 3145728 | tf_op jit(solution)/shard_map/pallas_call | solution.py:241
  25.0 0.5 %collective-permute-start.3 = (f32[8,8,256]{2,1,0:T(8,128)S(1)}, f32[8,8,256]{2,1,0:T(8,128)S(1)}, u32[]{:S(2)}, u32[]{:S(2)}) collective-permute-start(f32[8,8,256]{2,1,0:T(8,128)S(1)} %get-tuple-element.17), channel_id=1, source_target_pairs={{255,0},{224,1},{225,2},{226,3},{227,4},{228,5},{229,6},{230,7},{2... | collective-permute-start | bytes 196616 | tf_op jit(solution)/shard_map/ppermute | solution.py:193
  25.5 3.6 %collective-permute-start.4 = (f32[8,8,256]{2,1,0:T(8,128)S(1)}, f32[8,8,256]{2,1,0:T(8,128)S(1)}, u32[]{:S(2)}, u32[]{:S(2)}) collective-permute-start(f32[8,8,256]{2,1,0:T(8,128)S(1)} %get-tuple-element.18), channel_id=1, source_target_pairs={{224,0},{0,32},{32,64},{64,96},{96,128},{128,160},{160,192},{192,2... | collective-permute-start | bytes 196616 | tf_op jit(solution)/shard_map/ppermute | solution.py:187
  29.1 0.0 collective-permute-start.5
  29.1 4.2 %collective-permute-done.3 = f32[8,8,256]{2,1,0:T(8,128)S(1)} collective-permute-done((f32[8,8,256]{2,1,0:T(8,128)S(1)}, f32[8,8,256]{2,1,0:T(8,128)S(1)}, u32[]{:S(2)}, u32[]{:S(2)}) %collective-permute-start.3) | collective-permute-done | bytes 65568 | tf_op jit(solution)/shard_map/ppermute | solution.py:193
  33.3 0.0 collective-permute-done.4
  33.3 3.1 %collective-permute-done.5 = f32[8,8,256]{2,1,0:T(8,128)S(1)} collective-permute-done((f32[8,8,256]{2,1,0:T(8,128)S(1)}, f32[8,8,256]{2,1,0:T(8,128)S(1)}, u32[]{:S(2)}, u32[]{:S(2)}) %collective-permute-start.5) | collective-permute-done | bytes 65568 | tf_op jit(solution)/shard_map/ppermute | solution.py:185
  36.4 0.7 %maximum_maximum_fusion = f32[16,16,256]{2,1,0:T(8,128)} fusion(f32[8,8,256]{2,1,0:T(8,128)S(1)} %get-tuple-element.20, f32[8,8,256]{2,1,0:T(8,128)S(1)} %collective-permute-done.5, f32[8,8,256]{2,1,0:T(8,128)S(1)} %collective-permute-done.4, f32[8,8,256]{2,1,0:T(8,128)S(1)} %collective-permute-done.3), kind=kLoop, calls=%fused_computation | loop fusion | flops 196608 | bytes 524288 | tf_op jit(solution)/shard_map/concatenate | solution.py:255
  (12 shorter events, 0.0 us)
Async XLA Ops:
  0.0 17.3 %copy-start.5 = (f32[2,8,961]{2,1,0:T(8,128)S(1)}, f32[2,8,961]{2,1,0:T(8,128)}, u32[]{:S(2)}) copy-start(f32[2,8,961]{2,1,0:T(8,128)} %table.1) | copy-start | bytes 184516
  0.0 17.3 %copy-start.4 = (s32[256,256]{1,0:T(8,128)S(1)}, s32[256,256]{1,0:T(8,128)}, u32[]{:S(2)}) copy-start(s32[256,256]{1,0:T(8,128)} %index.1) | copy-start | bytes 786436
  0.0 17.3 %copy-start.9 = (s32[16,16]{1,0:T(8,128)S(1)}, s32[16,16]{1,0:T(8,128)}, u32[]{:S(2)}) copy-start(s32[16,16]{1,0:T(8,128)} %region.1) | copy-start | bytes 3076
  8.3 13.2 %copy-start = (bf16[2,256,1024]{2,1,0:T(8,128)(2,1)S(1)}, bf16[2,256,1024]{2,1,0:T(8,128)(2,1)}, u32[]{:S(2)}) copy-start(bf16[2,256,1024]{2,1,0:T(8,128)(2,1)} %wexpand.1) | copy-start | bytes 3145732
  8.3 13.2 %copy-start.1 = (bf16[2,1024,256]{2,1,0:T(8,128)(2,1)S(1)}, bf16[2,1024,256]{2,1,0:T(8,128)(2,1)}, u32[]{:S(2)}) copy-start(bf16[2,1024,256]{2,1,0:T(8,128)(2,1)} %wreduce.1) | copy-start | bytes 3145732
  8.4 13.2 %copy-start.2 = (bf16[2,256,768]{2,1,0:T(8,128)(2,1)S(1)}, bf16[2,256,768]{2,1,0:T(8,128)(2,1)}, u32[]{:S(2)}) copy-start(bf16[2,256,768]{2,1,0:T(8,128)(2,1)} %wqkv.1) | copy-start | bytes 2359300
  8.4 13.2 %copy-start.3 = (bf16[2,256,256]{2,1,0:T(8,128)(2,1)S(1)}, bf16[2,256,256]{2,1,0:T(8,128)(2,1)}, u32[]{:S(2)}) copy-start(bf16[2,256,256]{2,1,0:T(8,128)(2,1)} %wproj.1) | copy-start | bytes 786436
  8.4 13.2 %copy-start.6 = (f32[8,8,256]{2,1,0:T(8,128)S(1)}, f32[8,8,256]{2,1,0:T(8,128)}, u32[]{:S(2)}) copy-start(f32[8,8,256]{2,1,0:T(8,128)} %get-tuple-element.13.in00) | copy-start | bytes 196612
  8.4 13.2 %copy-start.7 = (f32[2,2,256]{2,1,0:T(2,128)S(1)}, f32[2,2,256]{2,1,0:T(2,128)}, u32[]{:S(2)}) copy-start(f32[2,2,256]{2,1,0:T(2,128)} %gain.1) | copy-start | bytes 12292
  8.4 13.2 %copy-start.8 = (f32[2,2,256]{2,1,0:T(2,128)S(1)}, f32[2,2,256]{2,1,0:T(2,128)}, u32[]{:S(2)}) copy-start(f32[2,2,256]{2,1,0:T(2,128)} %shift.1) | copy-start | bytes 12292
  8.4 12.1 %collective-permute-start = (f32[8,8,256]{2,1,0:T(8,128)}, f32[8,8,256]{2,1,0:T(8,128)S(1)}, u32[]{:S(2)}, u32[]{:S(2)}) collective-permute-start(f32[8,8,256]{2,1,0:T(8,128)} %get-tuple-element.14), channel_id=1, source_target_pairs={{1,0},{2,1},{3,2},{4,3},{5,4},{6,5},{7,6},{8,7},{9,8},{10,9},{11,1... | collective-permute-start | bytes 196616 | tf_op jit(solution)/shard_map/ppermute | solution.py:185
  16.4 5.1 %collective-permute-start.1 = (f32[8,8,256]{2,1,0:T(8,128)}, f32[8,8,256]{2,1,0:T(8,128)S(1)}, u32[]{:S(2)}, u32[]{:S(2)}) collective-permute-start(f32[8,8,256]{2,1,0:T(8,128)} %get-tuple-element.15), channel_id=1, source_target_pairs={{32,0},{64,32},{96,64},{128,96},{160,128},{192,160},{224,192},{0,2... | collective-permute-start | bytes 196616 | tf_op jit(solution)/shard_map/ppermute | solution.py:187
  17.0 4.6 %collective-permute-start.2 = (f32[8,8,256]{2,1,0:T(8,128)}, f32[8,8,256]{2,1,0:T(8,128)S(1)}, u32[]{:S(2)}, u32[]{:S(2)}) collective-permute-start(f32[8,8,256]{2,1,0:T(8,128)} %get-tuple-element.16), channel_id=1, source_target_pairs={{33,0},{34,1},{35,2},{36,3},{37,4},{38,5},{39,6},{40,7},{41,8},{42... | collective-permute-start | bytes 196616 | tf_op jit(solution)/shard_map/ppermute | solution.py:193
  25.0 8.3 %collective-permute-start.3 = (f32[8,8,256]{2,1,0:T(8,128)S(1)}, f32[8,8,256]{2,1,0:T(8,128)S(1)}, u32[]{:S(2)}, u32[]{:S(2)}) collective-permute-start(f32[8,8,256]{2,1,0:T(8,128)S(1)} %get-tuple-element.17), channel_id=1, source_target_pairs={{255,0},{224,1},{225,2},{226,3},{227,4},{228,5},{229,6},{230,7},{2... | collective-permute-start | bytes 196616 | tf_op jit(solution)/shard_map/ppermute | solution.py:193
  25.5 7.8 %collective-permute-start.4 = (f32[8,8,256]{2,1,0:T(8,128)S(1)}, f32[8,8,256]{2,1,0:T(8,128)S(1)}, u32[]{:S(2)}, u32[]{:S(2)}) collective-permute-start(f32[8,8,256]{2,1,0:T(8,128)S(1)} %get-tuple-element.18), channel_id=1, source_target_pairs={{224,0},{0,32},{32,64},{64,96},{96,128},{128,160},{160,192},{192,2... | collective-permute-start | bytes 196616 | tf_op jit(solution)/shard_map/ppermute | solution.py:187
  29.1 7.3 %collective-permute-start.5 = (f32[8,8,256]{2,1,0:T(8,128)S(1)}, f32[8,8,256]{2,1,0:T(8,128)S(1)}, u32[]{:S(2)}, u32[]{:S(2)}) collective-permute-start(f32[8,8,256]{2,1,0:T(8,128)S(1)} %get-tuple-element.19), channel_id=1, source_target_pairs={{31,0},{0,1},{1,2},{2,3},{3,4},{4,5},{5,6},{6,7},{7,8},{8,9},{9,10... | collective-permute-start | bytes 196616 | tf_op jit(solution)/shard_map/ppermute | solution.py:185

commit v2 on v1

v2 whole, which is shorter than its diff:
```python
import functools
import math

import jax
import jax.numpy as jnp
from jax import lax
from jax.experimental import pallas as pl
from jax.experimental.pallas import tpu as pltpu
from jax.sharding import PartitionSpec as P

HEADS = 8
LOG2E = math.log2(math.e)
ENTRIES = 961
FIXED = 8000.0
F32 = jnp.float32
BF16 = jnp.bfloat16


def take_lanes(x, lanes):
    return jnp.take_along_axis(x, lanes, axis=1, mode="promise_in_bounds")


def fill_lookup(table, lookup_ref):
    table = jnp.concatenate([table, jnp.zeros((HEADS, 1024 - ENTRIES), F32)], 1)
    fixed = jnp.round(table * FIXED).astype(jnp.int32)
    for pair in range(HEADS // 2):
        packed = (fixed[2 * pair : 2 * pair + 1] << 16) + fixed[2 * pair + 1 : 2 * pair + 2]
        for chunk in range(8):
            lookup_ref[pair * 8 + chunk] = jnp.broadcast_to(
                packed[:, chunk * 128 : chunk * 128 + 128], (8, 128)
            )


def look_up_tile(lookup_ref, index_ref, bias_ref, pair, row, half):
    scale = LOG2E / FIXED / 65536
    lanes = slice(half * 128, half * 128 + 128)
    index = index_ref[pl.ds(row, 8), lanes]
    low = index & 127
    found = [take_lanes(lookup_ref[pair * 8 + chunk], low) for chunk in range(8)]
    for bit in (128, 256, 512):
        odd = (index & bit) != 0
        found = [jnp.where(odd, found[2 * i + 1], found[2 * i]) for i in range(len(found) // 2)]
    bias_ref[2 * pair, pl.ds(row, 8), lanes] = found[0].astype(F32) * scale
    bias_ref[2 * pair + 1, pl.ds(row, 8), lanes] = (found[0] << 16).astype(F32) * scale


def look_up_bias(lookup_ref, index_ref, bias_ref, rows=4):
    def step(i, carry):
        for sub in range(rows):
            row = pl.multiple_of(i * (8 * rows) + sub * 8, 8)
            for half in range(2):
                for pair in range(HEADS // 2):
                    look_up_tile(lookup_ref, index_ref, bias_ref, pair, row, half)
        return carry

    lax.fori_loop(0, 32 // rows, step, 0)


def layer_norm(x, gain, shift):
    center = x - jnp.mean(x, -1, keepdims=True)
    spread = jnp.mean(center * center, -1, keepdims=True)
    return (center * lax.rsqrt(spread + 1e-05) * gain + shift).astype(BF16)


AHEAD = 2
EARLY = 64
EACH = 32


def attend(items, score, finish, beside=None):
    items = list(items)
    scores, raw = {}, {}
    for i in range(len(items) + AHEAD + 1):
        if i < len(items):
            scores[i] = score(items[i])
        if beside is not None:
            beside(i)
        if 0 <= i - AHEAD < len(items):
            now = scores.pop(i - AHEAD)
            raw[i - AHEAD] = jnp.exp2(now - jnp.max(now, 0, keepdims=True)).astype(BF16)
        if i - AHEAD >= 1:
            finish(items[i - AHEAD - 1], raw.pop(i - AHEAD - 1))


def attention(x, normed, bias_ref, wqkv, wproj, joined_ref, beside):
    query = jnp.dot(normed, wqkv[:, 0:256], preferred_element_type=F32)
    query = (query * (LOG2E / math.sqrt(32.0))).astype(BF16)
    keys = jnp.dot(normed, wqkv[:, 256:512], preferred_element_type=F32).astype(BF16)
    values = jnp.dot(normed, wqkv[:, 512:768], preferred_element_type=F32).T.astype(BF16)
    ones = jnp.ones((16, 256), BF16)
    head_of_lane = lax.broadcasted_iota(jnp.int32, (1, 128), 1) // 32

    def score(h):
        group = slice((h // 4) * 128, (h // 4) * 128 + 128)
        own = jnp.where(head_of_lane == h % 4, 1.0, 0.0).astype(BF16)
        scores = lax.dot_general(
            keys[:, group], query[:, group] * own, (((1,), (1,)), ((), ())), preferred_element_type=F32
        )
        return scores + bias_ref[h]

    def finish(h, raw):
        left = jnp.concatenate([values[32 * h : 32 * h + 32], ones], 0)
        out = jnp.dot(left, raw, preferred_element_type=F32)
        inverse = 1.0 / out[32:40]
        for j in range(2):
            part = jnp.concatenate(
                [out[16 * j : 16 * j + 8] * inverse, out[16 * j + 8 : 16 * j + 16] * inverse], 0
            )
            joined_ref[32 * h + 16 * j : 32 * h + 16 * j + 16, :] = part.astype(BF16)

    attend(range(HEADS), score, finish, beside)
    return x + lax.dot_general(
        joined_ref[...], wproj[...], (((0,), (0,)), ((), ())), preferred_element_type=F32
    )


def feed_forward(attended, normed, wexpand, wreduce):
    total = attended
    for j in range(4):
        part = slice(j * 256, j * 256 + 256)
        hidden = jnp.dot(normed, wexpand[:, part], preferred_element_type=F32)
        hidden = (hidden * (0.5 * lax.erf(hidden * math.sqrt(0.5)) + 0.5)).astype(BF16)
        total = total + jnp.dot(hidden, wreduce[part, :], preferred_element_type=F32)
    return total


def cell_order(x):
    return jnp.swapaxes(x.reshape(2, 8, 2, 8, x.shape[-1]), 1, 2).reshape(x.shape)


def from_cell_order(x):
    return jnp.swapaxes(x.reshape(2, 2, 8, 8, x.shape[-1]), 1, 2).reshape(x.shape)


def label_row(region):
    labels = region.astype(F32).astype(BF16)
    lane = lax.broadcasted_iota(jnp.int32, (16, 256), 1)
    row = lax.broadcasted_iota(jnp.int32, (16, 256), 0)
    i = (lane // 128) * 8 + (lane // 8) % 8
    j = (lane // 64) % 2 * 8 + lane % 8
    pick_col = jnp.where(j == row, 1.0, 0.0).astype(BF16)
    wide = jnp.dot(labels, pick_col, preferred_element_type=F32)
    return jnp.sum(jnp.where(i == row, wide, 0.0), 0, keepdims=True)


def first_kernel(
    x_hbm, index_hbm, region_hbm, table_hbm, gain_hbm, shift_hbm, wqkv_hbm, wproj_hbm, wexpand_hbm, wreduce_hbm,
    out, top, bottom,
    x, index, region, table, gain, shift, wqkv, wproj, wexpand, wreduce, lookup, index_t, bias, joined, sems,
):
    moves = [
        (index_hbm, index), (table_hbm.at[0], table), (x_hbm, x), (gain_hbm, gain), (shift_hbm, shift),
        (wqkv_hbm.at[0], wqkv), (wproj_hbm.at[0], wproj), (region_hbm, region), (wexpand_hbm.at[0], wexpand),
        (wreduce_hbm.at[0], wreduce),
    ]
    copies = [pltpu.make_async_copy(src, dst, sems.at[i]) for i, (src, dst) in enumerate(moves)]
    for copy in copies:
        copy.start()
    copies[0].wait()
    copies[1].wait()
    index_t[...] = index[...].T
    fill_lookup(table[...], lookup)

    def look_up(tiles):
        for pair, tile in tiles:
            look_up_tile(lookup, index_t, bias, pair, tile // 2 * 8, tile % 2)

    tiles = [(pair, tile) for pair in range(HEADS // 2) for tile in range(64)]
    look_up(tiles[:EARLY])
    for copy in copies[2:8]:
        copy.wait()
    bottom[128:136, :] = jnp.broadcast_to(label_row(region[...]), (8, 256))
    tile = x[...].reshape(256, 256)
    normed = layer_norm(tile, gain[0, 0:1], shift[0, 0:1])
    attended = attention(
        tile, normed, bias, wqkv, wproj, joined,
        lambda i: look_up(tiles[EARLY + i * EACH : EARLY + i * EACH + EACH]),
    )
    copies[8].wait()
    copies[9].wait()
    normed = layer_norm(attended, gain[0, 1:2], shift[0, 1:2])
    total = feed_forward(attended, normed, wexpand, wreduce)
    out[...] = total
    normed = layer_norm(total, gain[1, 0:1], shift[1, 0:1]).astype(F32)
    top[...] = normed[0:128]
    bottom[0:128, :] = normed[128:256]


def side_of(ref, side):
    return ref[0:128, :].reshape(8, 2, 8, 256)[:, side].reshape(64, 256)


def bias_kernel(index, table, top, bottom, bias, own_west, own_east, lookup, index_t):
    for side, strip in enumerate((own_west, own_east)):
        strip[0:64, :] = side_of(top, side)
        strip[64:128, :] = side_of(bottom, side)
    cells = index[...].reshape(2, 8, 2, 8, 256)
    queries = jnp.concatenate(
        [cells[1 - a, :, 1 - b].reshape(64, 256) for a in range(2) for b in range(2)], 0
    )
    index_t[...] = cell_order(queries.T)
    fill_lookup(table[1], lookup)
    look_up_bias(lookup, index_t, bias)


def join_kernel(north, south, bottom, own_west, own_east, to_west, to_east):
    for side, own, strip in ((0, own_west, to_west), (1, own_east, to_east)):
        strip[0:64, :] = side_of(north, side)
        strip[64:192, :] = own[...]
        strip[192:256, :] = side_of(south, side)
    to_east[256:257, :] = bottom[128:129, :]
    to_east[257:264, :] = north[128:135, :]


def second_kernel(
    x, top, bottom, north, south, west, east, bias, gain, shift, wqkv, wproj, wexpand, wreduce,
    out,
    around, keys, values, mask, joined,
):
    def pieces(ref, rows):
        return ref[0:rows, :].reshape(rows // 16, 2, 8, 256)

    upper = [pieces(north, 128), pieces(top, 128), pieces(bottom, 128), pieces(south, 128)]
    sides = [west[0:256, :], east[0:256, :]]
    for grid_row in range(4):
        for grid_col in range(4):
            if grid_col in (1, 2):
                cell = upper[grid_row][:, grid_col - 1].reshape(64, 256)
            else:
                cell = sides[grid_col // 3][grid_row * 64 : grid_row * 64 + 64]
            window = grid_row // 2 * 2 + grid_col // 2
            place = (grid_row % 2 * 2 + grid_col % 2) * 64
            around[window, place : place + 64, :] = cell.astype(BF16)

    labels = jnp.concatenate(
        [west[257:258, :], north[128:129, :], west[256:257, :], bottom[128:129, :]], 0
    )
    lane_window = lax.broadcasted_iota(jnp.int32, (4, 256), 1) // 64
    window_row = lax.broadcasted_iota(jnp.int32, (4, 256), 0)
    own_window = lane_window == window_row
    key_label = lax.dot_general(
        labels.astype(BF16), jnp.where(own_window, 1.0, 0.0).astype(BF16), (((0,), (0,)), ((), ())),
        preferred_element_type=F32,
    )
    turned = jnp.concatenate(
        [labels[t : t + 1, (3 - t) * 64 : (4 - t) * 64] for t in range(4)], 1
    )
    mask[...] = jnp.where(key_label == turned, 0.0, -jnp.inf)

    wqkv = wqkv.at[1]
    for window in range(4):
        tokens = around[window]
        key = jnp.dot(tokens, wqkv[:, 256:512], preferred_element_type=F32).astype(BF16)
        value = jnp.dot(tokens, wqkv[:, 512:768], preferred_element_type=F32).T.astype(BF16)
        for group in range(2):
            keys[group, window // 2, :, window % 2 * 128 : window % 2 * 128 + 128] = key[
                :, group * 128 : group * 128 + 128
            ]
        for h in range(HEADS):
            values[h, window // 2, window % 2 * 32 : window % 2 * 32 + 32, :] = value[h * 32 : h * 32 + 32]
    own = jnp.concatenate([around[t, (3 - t) * 64 : (4 - t) * 64, :] for t in range(4)], 0)
    query = jnp.dot(own, wqkv[:, 0:256], preferred_element_type=F32)
    query = (query * (LOG2E / math.sqrt(32.0))).astype(BF16)

    row = lax.broadcasted_iota(jnp.int32, (128, 256), 0)
    lane = lax.broadcasted_iota(jnp.int32, (128, 256), 1)
    left_cell = lax.broadcasted_iota(jnp.int32, (8, 128), 1) < 64
    ones = jnp.ones((16, 256), BF16)

    def score(item):
        h, half = item
        pick = jnp.where((row // 64 == lane // 128) & (lane % 128 // 32 == h % 4), 1.0, 0.0).astype(BF16)
        group = h // 4
        lanes = slice(half * 128, half * 128 + 128)
        part = query[lanes, group * 128 : group * 128 + 128]
        scores = lax.dot_general(
            keys[group, half], jnp.concatenate([part, part], 1) * pick, (((1,), (1,)), ((), ())),
            preferred_element_type=F32,
        )
        return scores + (bias[h, :, lanes] + mask[:, lanes])

    def finish(item, raw):
        h, half = item
        lanes = slice(half * 128, half * 128 + 128)
        left = jnp.concatenate([values[h, half], ones], 0)
        sums = jnp.dot(left, raw, preferred_element_type=F32)
        inverse = 1.0 / sums[64:72]
        for j in range(2):
            rows = [
                jnp.where(left_cell, sums[at : at + 8], sums[at + 32 : at + 40]) * inverse
                for at in (16 * j, 16 * j + 8)
            ]
            joined[32 * h + 16 * j : 32 * h + 16 * j + 16, lanes] = jnp.concatenate(rows, 0).astype(BF16)

    attend([(h, half) for h in range(HEADS) for half in range(2)], score, finish)
    attended = cell_order(x[...]) + lax.dot_general(
        joined[...], wproj[1], (((0,), (0,)), ((), ())), preferred_element_type=F32
    )
    normed = layer_norm(attended, gain[1, 1:2], shift[1, 1:2])
    total = feed_forward(attended, normed, wexpand.at[1], wreduce.at[1])
    out[...] = from_cell_order(total).reshape(16, 16, 256)


def shifted(x, axis, size, by):
    return lax.ppermute(x, axis, [((i + by) % size, i) for i in range(size)])


HBM = pl.BlockSpec(memory_space=pltpu.HBM)
VMEM = pl.BlockSpec(memory_space=pltpu.VMEM)


def cost(megabytes):
    return pl.CostEstimate(flops=10**9, bytes_accessed=megabytes << 20, transcendentals=0)


def call_first(*args):
    return pl.pallas_call(
        first_kernel,
        out_shape=[
            jax.ShapeDtypeStruct((256, 256), F32),
            jax.ShapeDtypeStruct((128, 256), F32),
            jax.ShapeDtypeStruct((136, 256), F32),
        ],
        in_specs=[HBM] * 10,
        out_specs=[VMEM] * 3,
        scratch_shapes=[
            pltpu.VMEM((16, 16, 256), F32),
            pltpu.VMEM((256, 256), jnp.int32),
            pltpu.VMEM((16, 16), jnp.int32),
            pltpu.VMEM((HEADS, ENTRIES), F32),
            pltpu.VMEM((2, 2, 256), F32),
            pltpu.VMEM((2, 2, 256), F32),
            pltpu.VMEM((256, 768), BF16),
            pltpu.VMEM((256, 256), BF16),
            pltpu.VMEM((256, 1024), BF16),
            pltpu.VMEM((1024, 256), BF16),
            pltpu.VMEM((32, 8, 128), jnp.int32),
            pltpu.VMEM((256, 256), jnp.int32),
            pltpu.VMEM((HEADS, 256, 256), F32),
            pltpu.VMEM((256, 256), BF16),
            pltpu.SemaphoreType.DMA((10,)),
        ],
        compiler_params=pltpu.CompilerParams(vmem_limit_bytes=40 << 20),
        cost_estimate=cost(3),
    )(*args)


def call_bias(*args):
    return pl.pallas_call(
        bias_kernel,
        out_shape=[
            jax.ShapeDtypeStruct((HEADS, 256, 256), F32),
            jax.ShapeDtypeStruct((128, 256), F32),
            jax.ShapeDtypeStruct((128, 256), F32),
        ],
        in_specs=[VMEM] * 4,
        out_specs=[VMEM] * 3,
        scratch_shapes=[
            pltpu.VMEM((32, 8, 128), jnp.int32),
            pltpu.VMEM((256, 256), jnp.int32),
        ],
        compiler_params=pltpu.CompilerParams(vmem_limit_bytes=16 << 20),
        cost_estimate=cost(8),
    )(*args)


def call_join(*args):
    return pl.pallas_call(
        join_kernel,
        out_shape=[jax.ShapeDtypeStruct((256, 256), F32), jax.ShapeDtypeStruct((264, 256), F32)],
        in_specs=[VMEM] * 5,
        out_specs=[VMEM] * 2,
        compiler_params=pltpu.CompilerParams(vmem_limit_bytes=4 << 20),
        cost_estimate=cost(1),
    )(*args)


def call_second(*args):
    return pl.pallas_call(
        second_kernel,
        out_shape=jax.ShapeDtypeStruct((16, 16, 256), F32),
        in_specs=[VMEM] * 14,
        out_specs=VMEM,
        scratch_shapes=[
            pltpu.VMEM((4, 256, 256), BF16),
            pltpu.VMEM((2, 2, 256, 256), BF16),
            pltpu.VMEM((HEADS, 2, 64, 256), BF16),
            pltpu.VMEM((256, 256), F32),
            pltpu.VMEM((256, 256), BF16),
        ],
        compiler_params=pltpu.CompilerParams(vmem_limit_bytes=16 << 20),
        cost_estimate=cost(3),
    )(*args)


def per_device(rows, cols, tokens, region, index, gain, shift, wqkv, wproj, wexpand, wreduce, table):
    resting = [
        pltpu.with_memory_space_constraint(v, pltpu.HBM)
        for v in (tokens, index, region, table, gain, shift, wqkv, wproj, wexpand, wreduce)
    ]
    first, top, bottom = call_first(*resting)
    north = shifted(bottom, "row", rows, -1)
    south = shifted(top, "row", rows, 1)
    bias, own_west, own_east = call_bias(index, table, top, bottom)
    to_west, to_east = call_join(north, south, bottom, own_west, own_east)
    west = shifted(to_east, "col", cols, -1)
    east = shifted(to_west, "col", cols, 1)
    return call_second(
        first, top, bottom, north, south, west, east, bias, gain, shift, wqkv, wproj, wexpand, wreduce
    )


def solution(mesh):
    in_specs = (P("row", "col", None), P("row", "col"), P(), P(), P(), P(), P(), P(), P(), P())
    body = functools.partial(per_device, mesh.shape["row"], mesh.shape["col"])
    return jax.shard_map(
        body, mesh=mesh, in_specs=in_specs, out_specs=P("row", "col", None), check_vma=False
    )
```

time: 37.2 us -> 28.8 us (0.77)
  the two profiles are of different devices: /device:TPU:4 before, /device:TPU:103 now
where the time goes in v2:
time: 28.8 us; the launch traced here: 28.7 us
  Pallas kernels  13.1 us (45%)
  waiting for transfers between devices  8.9 us (31%)
  starting transfers between devices  6.47 us (22%)
    ppermute x4, waiting for transfers between devices, shifted(): return lax.ppermute(x, axis, [((i + by) % size, i) for i in range(size)])  8.9 us
    ppermute x4, starting transfers between devices, shifted(): return lax.ppermute(x, axis, [((i + by) % size, i) for i in range(size)])  6.47 us
    pallas_call x1, Pallas kernels, call_first(): pl.pallas_call(first_kernel, out_shape=[jax.ShapeDtypeStruct((256, 256),...  5.99 us
    pallas_call x1, Pallas kernels, call_bias(): pl.pallas_call(bias_kernel, out_shape=[jax.ShapeDtypeStruct((HEADS, 256,...  3.7 us
    pallas_call x1, Pallas kernels, call_second(): pl.pallas_call(second_kernel, out_shape=jax.ShapeDtypeStruct((16, 16, 256...  3.42 us
  transfers between devices with their start and end apart: 4, of which 2 were waited for; matrix products, arithmetic and copies ran while one was open for 0% of the time, Pallas kernels for 13%

profile of v2, /device:TPU:103, one launch (start us, length us, event | category | flops | bytes accessed | tf_op | source)
XLA Modules:
  0.0 28.7 jit_solution(12957304903220909382)
XLA Ops:
  0.0 6.0 %shard_map.100 = (f32[256,256]{1,0:T(8,128)S(1)}, f32[128,256]{1,0:T(8,128)S(1)}, f32[136,256]{1,0:T(8,128)S(1)}) custom-call(f32[16,16,256]{2,1,0:T(8,128)} %x_hbm.1, s32[256,256]{1,0:T(8,128)} %index.1, s32[16,16]{1,0:T(8,128)} %region_hbm.1, f32[2,8,961]{2,1,0:T(8,128)} %table.1, f32[2,2,256]{2,1,0:T(2,128)} %gain.1, f32[2,2,256]{2,1,0:T(2,128)} %shift.1, ...), custom_call_target="tpu_custom_call" | custom-call | flops 1000000000 | bytes 3145728 | tf_op jit(solution)/shard_map/pallas_call | solution.py:317
  6.0 1.3 %collective-permute-start = (f32[136,256]{1,0:T(8,128)S(1)}, f32[136,256]{1,0:T(8,128)S(1)}, u32[]{:S(2)}, u32[]{:S(2)}) collective-permute-start(f32[136,256]{1,0:T(8,128)S(1)} %get-tuple-element.15.bottom), channel_id=1, source_target_pairs={{224,0},{0,32},{32,64},{64,96},{96,128},{128,160},{160,192},{192,2... | collective-permute-start | bytes 417800 | tf_op jit(solution)/shard_map/ppermute | solution.py:305
  7.3 0.3 collective-permute-start.1
  7.5 0.0 copy-done.5
  7.5 0.0 copy-done.4
  7.5 3.7 %shard_map.101 = (f32[8,256,256]{2,1,0:T(8,128)S(1)}, f32[128,256]{1,0:T(8,128)S(1)}, f32[128,256]{1,0:T(8,128)S(1)}) custom-call(s32[256,256]{1,0:T(8,128)S(1)} %copy-done.4, f32[2,8,961]{2,1,0:T(8,128)S(1)} %copy-done.5, f32[128,256]{1,0:T(8,128)S(1)} %get-tuple-element.14.top, f32[136,256]{1,0:T(8,128)S(1)} %get-tuple-element.15.bottom), custom_call_target="tpu_custom_call" | custom-call | flops 1000000000 | bytes 8388608 | tf_op jit(solution)/shard_map/pallas_call | solution.py:349
  11.3 0.0 copy-start
  11.3 0.0 copy-start.1
  11.3 0.0 copy-start.2
  11.3 0.0 copy-start.3
  11.3 0.0 copy-start.6
  11.3 0.0 copy-start.7
  11.3 1.9 %collective-permute-done.1.south = f32[128,256]{1,0:T(8,128)S(1)} collective-permute-done((f32[128,256]{1,0:T(8,128)S(1)}, f32[128,256]{1,0:T(8,128)S(1)}, u32[]{:S(2)}, u32[]{:S(2)}) %collective-permute-start.1) | collective-permute-done | bytes 131104 | tf_op jit(solution)/shard_map/ppermute | solution.py:305
  13.2 0.0 collective-permute-done.north
  13.3 4.9 %collective-permute-start.2 = (f32[264,256]{1,0:T(8,128)S(1)}, f32[264,256]{1,0:T(8,128)S(1)}, u32[]{:S(2)}, u32[]{:S(2)}) collective-permute-start(f32[264,256]{1,0:T(8,128)S(1)} %get-tuple-element.18), channel_id=1, source_target_pairs={{31,0},{0,1},{1,2},{2,3},{3,4},{4,5},{5,6},{6,7},{7,8},{8,9},{9,10... | collective-permute-start | bytes 811016 | tf_op jit(solution)/shard_map/ppermute | solution.py:305
  18.2 0.0 collective-permute-start.3
  18.2 7.0 %collective-permute-done.3.east = f32[256,256]{1,0:T(8,128)S(1)} collective-permute-done((f32[256,256]{1,0:T(8,128)S(1)}, f32[256,256]{1,0:T(8,128)S(1)}, u32[]{:S(2)}, u32[]{:S(2)}) %collective-permute-start.3) | collective-permute-done | bytes 262176 | tf_op jit(solution)/shard_map/ppermute | solution.py:305
  25.2 0.0 collective-permute-done.2.west
  25.2 0.0 copy-done
  25.2 0.0 copy-done.1
  25.2 0.0 copy-done.2
  25.2 0.0 copy-done.3
  25.2 0.0 copy-done.6
  25.2 3.4 %shard_map.103 = f32[16,16,256]{2,1,0:T(8,128)} custom-call(f32[256,256]{1,0:T(8,128)S(1)} %get-tuple-element.13.x, f32[128,256]{1,0:T(8,128)S(1)} %get-tuple-element.14.top, f32[136,256]{1,0:T(8,128)S(1)} %get-tuple-element.15.bottom, f32[136,256]{1,0:T(8,128)S(1)} %collective-permute-done.north, f32[128,256]{1,0:T(8,128)S(1)} %collective-permute-done.1.south, ...), custom_call_target="tpu_custom_call" | custom-call | flops 1000000000 | bytes 3145728 | tf_op jit(solution)/shard_map/pallas_call | solution.py:379
  (4 shorter events, 0.0 us)
Async XLA Ops:
  0.0 7.5 %copy-start.5 = (f32[2,8,961]{2,1,0:T(8,128)S(1)}, f32[2,8,961]{2,1,0:T(8,128)}, u32[]{:S(2)}) copy-start(f32[2,8,961]{2,1,0:T(8,128)} %table.1) | copy-start | bytes 184516
  0.0 7.5 %copy-start.4 = (s32[256,256]{1,0:T(8,128)S(1)}, s32[256,256]{1,0:T(8,128)}, u32[]{:S(2)}) copy-start(s32[256,256]{1,0:T(8,128)} %index.1) | copy-start | bytes 786436
  6.0 7.2 %collective-permute-start = (f32[136,256]{1,0:T(8,128)S(1)}, f32[136,256]{1,0:T(8,128)S(1)}, u32[]{:S(2)}, u32[]{:S(2)}) collective-permute-start(f32[136,256]{1,0:T(8,128)S(1)} %get-tuple-element.15.bottom), channel_id=1, source_target_pairs={{224,0},{0,32},{32,64},{64,96},{96,128},{128,160},{160,192},{192,2... | collective-permute-start | bytes 417800 | tf_op jit(solution)/shard_map/ppermute | solution.py:305
  7.3 5.9 %collective-permute-start.1 = (f32[128,256]{1,0:T(8,128)S(1)}, f32[128,256]{1,0:T(8,128)S(1)}, u32[]{:S(2)}, u32[]{:S(2)}) collective-permute-start(f32[128,256]{1,0:T(8,128)S(1)} %get-tuple-element.14.top), channel_id=1, source_target_pairs={{32,0},{64,32},{96,64},{128,96},{160,128},{192,160},{224,192},{0,2... | collective-permute-start | bytes 393224 | tf_op jit(solution)/shard_map/ppermute | solution.py:305
  11.3 13.9 %copy-start = (bf16[2,256,1024]{2,1,0:T(8,128)(2,1)S(1)}, bf16[2,256,1024]{2,1,0:T(8,128)(2,1)}, u32[]{:S(2)}) copy-start(bf16[2,256,1024]{2,1,0:T(8,128)(2,1)} %wexpand.1) | copy-start | bytes 3145732
  11.3 13.9 %copy-start.1 = (bf16[2,1024,256]{2,1,0:T(8,128)(2,1)S(1)}, bf16[2,1024,256]{2,1,0:T(8,128)(2,1)}, u32[]{:S(2)}) copy-start(bf16[2,1024,256]{2,1,0:T(8,128)(2,1)} %wreduce.1) | copy-start | bytes 3145732
  11.3 13.9 %copy-start.2 = (bf16[2,256,768]{2,1,0:T(8,128)(2,1)S(1)}, bf16[2,256,768]{2,1,0:T(8,128)(2,1)}, u32[]{:S(2)}) copy-start(bf16[2,256,768]{2,1,0:T(8,128)(2,1)} %wqkv.1) | copy-start | bytes 2359300
  11.3 13.9 %copy-start.3 = (bf16[2,256,256]{2,1,0:T(8,128)(2,1)S(1)}, bf16[2,256,256]{2,1,0:T(8,128)(2,1)}, u32[]{:S(2)}) copy-start(bf16[2,256,256]{2,1,0:T(8,128)(2,1)} %wproj.1) | copy-start | bytes 786436
  11.3 13.9 %copy-start.6 = (f32[2,2,256]{2,1,0:T(2,128)S(1)}, f32[2,2,256]{2,1,0:T(2,128)}, u32[]{:S(2)}) copy-start(f32[2,2,256]{2,1,0:T(2,128)} %gain.1) | copy-start | bytes 12292
  11.3 13.9 %copy-start.7 = (f32[2,2,256]{2,1,0:T(2,128)S(1)}, f32[2,2,256]{2,1,0:T(2,128)}, u32[]{:S(2)}) copy-start(f32[2,2,256]{2,1,0:T(2,128)} %shift.1) | copy-start | bytes 12292
  13.3 11.9 %collective-permute-start.2 = (f32[264,256]{1,0:T(8,128)S(1)}, f32[264,256]{1,0:T(8,128)S(1)}, u32[]{:S(2)}, u32[]{:S(2)}) collective-permute-start(f32[264,256]{1,0:T(8,128)S(1)} %get-tuple-element.18), channel_id=1, source_target_pairs={{31,0},{0,1},{1,2},{2,3},{3,4},{4,5},{5,6},{6,7},{7,8},{8,9},{9,10... | collective-permute-start | bytes 811016 | tf_op jit(solution)/shard_map/ppermute | solution.py:305
  18.2 7.0 %collective-permute-start.3 = (f32[256,256]{1,0:T(8,128)S(1)}, f32[256,256]{1,0:T(8,128)S(1)}, u32[]{:S(2)}, u32[]{:S(2)}) collective-permute-start(f32[256,256]{1,0:T(8,128)S(1)} %get-tuple-element.19), channel_id=1, source_target_pairs={{1,0},{2,1},{3,2},{4,3},{5,4},{6,5},{7,6},{8,7},{9,8},{10,9},{11,1... | collective-permute-start | bytes 786440 | tf_op jit(solution)/shard_map/ppermute | solution.py:305

commit v3 on v2

--- a/solution.py
+++ b/solution.py
@@ -11,7 +11,11 @@
 HEADS = 8
 LOG2E = math.log2(math.e)
 ENTRIES = 961
-FIXED = 8000.0
+WORDS = (
+    ((0, 11, 21), (1, 11, 10), (2, 10, 0)),
+    ((3, 11, 21), (4, 11, 10), (5, 10, 0)),
+    ((6, 16, 16), (7, 16, 0)),
+)
 F32 = jnp.float32
 BF16 = jnp.bfloat16
 
@@ -20,37 +24,46 @@
     return jnp.take_along_axis(x, lanes, axis=1, mode="promise_in_bounds")
 
 
+def field_scale(bits):
+    return (2 ** (bits - 1) - 1) / 4
+
+
 def fill_lookup(table, lookup_ref):
     table = jnp.concatenate([table, jnp.zeros((HEADS, 1024 - ENTRIES), F32)], 1)
-    fixed = jnp.round(table * FIXED).astype(jnp.int32)
-    for pair in range(HEADS // 2):
-        packed = (fixed[2 * pair : 2 * pair + 1] << 16) + fixed[2 * pair + 1 : 2 * pair + 2]
+    for at, word in enumerate(WORDS):
+        packed = 0
+        for head, bits, low in word:
+            fixed = jnp.round(table[head : head + 1] * field_scale(bits)).astype(jnp.int32)
+            packed = packed | ((fixed & (2**bits - 1)) << low)
         for chunk in range(8):
-            lookup_ref[pair * 8 + chunk] = jnp.broadcast_to(
+            lookup_ref[at * 8 + chunk] = jnp.broadcast_to(
                 packed[:, chunk * 128 : chunk * 128 + 128], (8, 128)
             )
 
 
-def look_up_tile(lookup_ref, index_ref, bias_ref, pair, row, half):
-    scale = LOG2E / FIXED / 65536
+def look_up_tile(lookup_ref, index_ref, bias_ref, words, row, half):
     lanes = slice(half * 128, half * 128 + 128)
     index = index_ref[pl.ds(row, 8), lanes]
-    low = index & 127
-    found = [take_lanes(lookup_ref[pair * 8 + chunk], low) for chunk in range(8)]
-    for bit in (128, 256, 512):
-        odd = (index & bit) != 0
-        found = [jnp.where(odd, found[2 * i + 1], found[2 * i]) for i in range(len(found) // 2)]
-    bias_ref[2 * pair, pl.ds(row, 8), lanes] = found[0].astype(F32) * scale
-    bias_ref[2 * pair + 1, pl.ds(row, 8), lanes] = (found[0] << 16).astype(F32) * scale
-
-
-def look_up_bias(lookup_ref, index_ref, bias_ref, rows=4):
+    low_index = index & 127
+    odd = [(index & bit) != 0 for bit in (128, 256, 512)]
+    for at in words:
+        found = [take_lanes(lookup_ref[at * 8 + chunk], low_index) for chunk in range(8)]
+        for bit in odd:
+            found = [jnp.where(bit, found[2 * i + 1], found[2 * i]) for i in range(len(found) // 2)]
+        for head, bits, low in WORDS[at]:
+            field = found[0]
+            if low + bits < 32:
+                field = field << (32 - low - bits)
+            field = field >> (32 - bits)
+            bias_ref[head, pl.ds(row, 8), lanes] = field.astype(F32) * (LOG2E / field_scale(bits))
+
+
+def look_up_bias(lookup_ref, index_ref, bias_ref, rows=32):
     def step(i, carry):
         for sub in range(rows):
             row = pl.multiple_of(i * (8 * rows) + sub * 8, 8)
             for half in range(2):
-                for pair in range(HEADS // 2):
-                    look_up_tile(lookup_ref, index_ref, bias_ref, pair, row, half)
+                look_up_tile(lookup_ref, index_ref, bias_ref, range(len(WORDS)), row, half)
         return carry
 
     lax.fori_loop(0, 32 // rows, step, 0)
@@ -64,20 +77,20 @@
 
 AHEAD = 2
 EARLY = 64
-EACH = 32
-
-
-def attend(items, score, finish, beside=None):
+EACH = 11
+
+
+def attend(items, score, finish, beside=lambda step: None):
     items = list(items)
     scores, raw = {}, {}
     for i in range(len(items) + AHEAD + 1):
         if i < len(items):
             scores[i] = score(items[i])
-        if beside is not None:
-            beside(i)
+        beside(2 * i)
         if 0 <= i - AHEAD < len(items):
             now = scores.pop(i - AHEAD)
             raw[i - AHEAD] = jnp.exp2(now - jnp.max(now, 0, keepdims=True)).astype(BF16)
+        beside(2 * i + 1)
         if i - AHEAD >= 1:
             finish(items[i - AHEAD - 1], raw.pop(i - AHEAD - 1))
 
@@ -162,10 +175,10 @@
     fill_lookup(table[...], lookup)
 
     def look_up(tiles):
-        for pair, tile in tiles:
-            look_up_tile(lookup, index_t, bias, pair, tile // 2 * 8, tile % 2)
-
-    tiles = [(pair, tile) for pair in range(HEADS // 2) for tile in range(64)]
+        for words, tile in tiles:
+            look_up_tile(lookup, index_t, bias, words, tile // 2 * 8, tile % 2)
+
+    tiles = [(words, tile) for words in ((0,), (1, 2)) for tile in range(64)]
     look_up(tiles[:EARLY])
     for copy in copies[2:8]:
         copy.wait()
@@ -198,7 +211,11 @@
     queries = jnp.concatenate(
         [cells[1 - a, :, 1 - b].reshape(64, 256) for a in range(2) for b in range(2)], 0
     )
-    index_t[...] = cell_order(queries.T)
+    keys = queries.T.reshape(2, 8, 2, 8, 256)
+    columns = [keys[:, :, c].reshape(128, 256) for c in range(2)]
+    right = lax.broadcasted_iota(jnp.int32, (128, 256), 1) // 64 % 2 == 1
+    index_t[0:128, :] = jnp.where(right, columns[0], columns[1])
+    index_t[128:256, :] = jnp.where(right, columns[1], columns[0])
     fill_lookup(table[1], lookup)
     look_up_bias(lookup, index_t, bias)
 
@@ -212,42 +229,7 @@
     to_east[257:264, :] = north[128:135, :]
 
 
-def second_kernel(
-    x, top, bottom, north, south, west, east, bias, gain, shift, wqkv, wproj, wexpand, wreduce,
-    out,
-    around, keys, values, mask, joined,
-):
-    def pieces(ref, rows):
-        return ref[0:rows, :].reshape(rows // 16, 2, 8, 256)
-
-    upper = [pieces(north, 128), pieces(top, 128), pieces(bottom, 128), pieces(south, 128)]
-    sides = [west[0:256, :], east[0:256, :]]
-    for grid_row in range(4):
-        for grid_col in range(4):
-            if grid_col in (1, 2):
-                cell = upper[grid_row][:, grid_col - 1].reshape(64, 256)
-            else:
-                cell = sides[grid_col // 3][grid_row * 64 : grid_row * 64 + 64]
-            window = grid_row // 2 * 2 + grid_col // 2
-            place = (grid_row % 2 * 2 + grid_col % 2) * 64
-            around[window, place : place + 64, :] = cell.astype(BF16)
-
-    labels = jnp.concatenate(
-        [west[257:258, :], north[128:129, :], west[256:257, :], bottom[128:129, :]], 0
-    )
-    lane_window = lax.broadcasted_iota(jnp.int32, (4, 256), 1) // 64
-    window_row = lax.broadcasted_iota(jnp.int32, (4, 256), 0)
-    own_window = lane_window == window_row
-    key_label = lax.dot_general(
-        labels.astype(BF16), jnp.where(own_window, 1.0, 0.0).astype(BF16), (((0,), (0,)), ((), ())),
-        preferred_element_type=F32,
-    )
-    turned = jnp.concatenate(
-        [labels[t : t + 1, (3 - t) * 64 : (4 - t) * 64] for t in range(4)], 1
-    )
-    mask[...] = jnp.where(key_label == turned, 0.0, -jnp.inf)
-
-    wqkv = wqkv.at[1]
+def project(around, wqkv, keys, values):
     for window in range(4):
         tokens = around[window]
         key = jnp.dot(tokens, wqkv[:, 256:512], preferred_element_type=F32).astype(BF16)
@@ -258,31 +240,78 @@
             ]
         for h in range(HEADS):
             values[h, window // 2, window % 2 * 32 : window % 2 * 32 + 32, :] = value[h * 32 : h * 32 + 32]
-    own = jnp.concatenate([around[t, (3 - t) * 64 : (4 - t) * 64, :] for t in range(4)], 0)
-    query = jnp.dot(own, wqkv[:, 0:256], preferred_element_type=F32)
-    query = (query * (LOG2E / math.sqrt(32.0))).astype(BF16)
-
+
+
+def cell_scores(keys, query, h, half):
     row = lax.broadcasted_iota(jnp.int32, (128, 256), 0)
     lane = lax.broadcasted_iota(jnp.int32, (128, 256), 1)
+    pick = jnp.where((row // 64 == lane // 128) & (lane % 128 // 32 == h % 4), 1.0, 0.0).astype(BF16)
+    group = h // 4
+    part = query[half * 128 : half * 128 + 128, group * 128 : group * 128 + 128]
+    return lax.dot_general(
+        keys[group, half], jnp.concatenate([part, part], 1) * pick, (((1,), (1,)), ((), ())),
+        preferred_element_type=F32,
+    )
+
+
+def early_kernel(top, bottom, north, south, bias, wqkv, scores, values, query, around, keys):
+    for grid_row, ref in enumerate((north, top, bottom, south)):
+        for b in range(2):
+            place = grid_row % 2 * 64
+            around[grid_row // 2 * 2 + b, place : place + 64, :] = side_of(ref, b).astype(BF16)
+    wqkv = wqkv.at[1]
+    project(around, wqkv, keys, values)
+    own = jnp.concatenate([around[t, (1 - t // 2) * 64 : (2 - t // 2) * 64, :] for t in range(4)], 0)
+    scaled = jnp.dot(own, wqkv[:, 0:256], preferred_element_type=F32)
+    query[...] = (scaled * (LOG2E / math.sqrt(32.0))).astype(BF16)
+    for h in range(HEADS):
+        for half in range(2):
+            lanes = slice(half * 128, half * 128 + 128)
+            scores[h, :, lanes] = cell_scores(keys, query, h, half) + bias[h, 0:128, lanes]
+
+
+def second_kernel(
+    x, bottom, north, west, east, bias, early_scores, early_values, query, gain, shift, wqkv, wproj, wexpand, wreduce,
+    out,
+    around, keys, values, mask, joined,
+):
+    for grid_row in range(4):
+        for b, ref in enumerate((west, east)):
+            place = grid_row % 2 * 64
+            cell = ref[grid_row * 64 : grid_row * 64 + 64, :]
+            around[grid_row // 2 * 2 + b, place : place + 64, :] = cell.astype(BF16)
+
+    labels = [west[257:258, :], north[128:129, :], west[256:257, :], bottom[128:129, :]]
+    order = ((1, 3, 0, 2), (0, 2, 1, 3))
+    labels = [
+        jnp.concatenate([labels[t][:, c * 64 : c * 64 + 64] for c in order[t % 2]], 1) for t in range(4)
+    ]
+    lane_window = lax.broadcasted_iota(jnp.int32, (4, 256), 1) // 64
+    window_row = lax.broadcasted_iota(jnp.int32, (4, 256), 0)
+    own_window = lane_window == window_row
+    key_label = lax.dot_general(
+        jnp.concatenate(labels, 0).astype(BF16), jnp.where(own_window, 1.0, 0.0).astype(BF16),
+        (((0,), (0,)), ((), ())), preferred_element_type=F32,
+    )
+    query_label = jnp.concatenate(
+        [labels[t][:, (1 - t // 2) * 64 : (2 - t // 2) * 64] for t in range(4)], 1
+    )
+    mask[...] = jnp.where(key_label == query_label, 0.0, -jnp.inf)
+
+    project(around, wqkv.at[1], keys, values)
     left_cell = lax.broadcasted_iota(jnp.int32, (8, 128), 1) < 64
     ones = jnp.ones((16, 256), BF16)
 
     def score(item):
         h, half = item
-        pick = jnp.where((row // 64 == lane // 128) & (lane % 128 // 32 == h % 4), 1.0, 0.0).astype(BF16)
-        group = h // 4
         lanes = slice(half * 128, half * 128 + 128)
-        part = query[lanes, group * 128 : group * 128 + 128]
-        scores = lax.dot_general(
-            keys[group, half], jnp.concatenate([part, part], 1) * pick, (((1,), (1,)), ((), ())),
-            preferred_element_type=F32,
-        )
-        return scores + (bias[h, :, lanes] + mask[:, lanes])
+        late = cell_scores(keys, query, h, half) + bias[h, 128:256, lanes]
+        return jnp.concatenate([early_scores[h, :, lanes], late], 0) + mask[:, lanes]
 
     def finish(item, raw):
         h, half = item
         lanes = slice(half * 128, half * 128 + 128)
-        left = jnp.concatenate([values[h, half], ones], 0)
+        left = jnp.concatenate([jnp.concatenate([early_values[h, half], values[h, half]], 1), ones], 0)
         sums = jnp.dot(left, raw, preferred_element_type=F32)
         inverse = 1.0 / sums[64:72]
         for j in range(2):
@@ -334,7 +363,7 @@
             pltpu.VMEM((256, 256), BF16),
             pltpu.VMEM((256, 1024), BF16),
             pltpu.VMEM((1024, 256), BF16),
-            pltpu.VMEM((32, 8, 128), jnp.int32),
+            pltpu.VMEM((24, 8, 128), jnp.int32),
             pltpu.VMEM((256, 256), jnp.int32),
             pltpu.VMEM((HEADS, 256, 256), F32),
             pltpu.VMEM((256, 256), BF16),
@@ -356,7 +385,7 @@
         in_specs=[VMEM] * 4,
         out_specs=[VMEM] * 3,
         scratch_shapes=[
-            pltpu.VMEM((32, 8, 128), jnp.int32),
+            pltpu.VMEM((24, 8, 128), jnp.int32),
             pltpu.VMEM((256, 256), jnp.int32),
         ],
         compiler_params=pltpu.CompilerParams(vmem_limit_bytes=16 << 20),
@@ -375,16 +404,35 @@
     )(*args)
 
 
+def call_early(*args):
+    return pl.pallas_call(
+        early_kernel,
+        out_shape=[
+            jax.ShapeDtypeStruct((HEADS, 128, 256), F32),
+            jax.ShapeDtypeStruct((HEADS, 2, 64, 128), BF16),
+            jax.ShapeDtypeStruct((256, 256), BF16),
+        ],
+        in_specs=[VMEM] * 6,
+        out_specs=[VMEM] * 3,
+        scratch_shapes=[
+            pltpu.VMEM((4, 128, 256), BF16),
+            pltpu.VMEM((2, 2, 128, 256), BF16),
+        ],
+        compiler_params=pltpu.CompilerParams(vmem_limit_bytes=16 << 20),
+        cost_estimate=cost(8),
+    )(*args)
+
+
 def call_second(*args):
     return pl.pallas_call(
         second_kernel,
         out_shape=jax.ShapeDtypeStruct((16, 16, 256), F32),
-        in_specs=[VMEM] * 14,
+        in_specs=[VMEM] * 15,
         out_specs=VMEM,
         scratch_shapes=[
-            pltpu.VMEM((4, 256, 256), BF16),
-            pltpu.VMEM((2, 2, 256, 256), BF16),
-            pltpu.VMEM((HEADS, 2, 64, 256), BF16),
+            pltpu.VMEM((4, 128, 256), BF16),
+            pltpu.VMEM((2, 2, 128, 256), BF16),
+            pltpu.VMEM((HEADS, 2, 64, 128), BF16),
             pltpu.VMEM((256, 256), F32),
             pltpu.VMEM((256, 256), BF16),
         ],
@@ -405,8 +453,10 @@
     to_west, to_east = call_join(north, south, bottom, own_west, own_east)
     west = shifted(to_east, "col", cols, -1)
     east = shifted(to_west, "col", cols, 1)
+    scores, values, query = call_early(top, bottom, north, south, bias, wqkv)
     return call_second(
-        first, top, bottom, north, south, west, east, bias, gain, shift, wqkv, wproj, wexpand, wreduce
+        first, bottom, north, west, east, bias, scores, values, query,
+        gain, shift, wqkv, wproj, wexpand, wreduce,
     )
 
 

time: 28.8 us -> 27.7 us (0.962)
  Pallas kernels: 13.1 us -> 11.2 us
  waiting for transfers between devices: 8.9 us -> 9.87 us
    pallas_call x1, Pallas kernels: 3.7 us -> 1.97 us  [call_bias(): pl.pallas_call(bias_kernel, out_shape=[jax.ShapeDtypeStruct((HEADS, 256,...]
    ppermute x4, waiting for transfers between devices: 8.9 us -> 9.87 us  [shifted(): return lax.ppermute(x, axis, [((i + by) % size, i) for i in range(size)])]
    pallas_call x1, Pallas kernels: 5.99 us -> 5.16 us  [call_first(): pl.pallas_call(first_kernel, out_shape=[jax.ShapeDtypeStruct((256, 256),...]
    pallas_call x0 -> x1, Pallas kernels: none -> 0.81 us  [call_early(): pl.pallas_call(early_kernel, out_shape=[jax.ShapeDtypeStruct((HEADS, 128,...]
  transfers between devices with their start and end apart: 4 -> 4, of which waited for: 2 -> 2; matrix products, arithmetic and copies ran while one was open for 0% -> 0% of each run, Pallas kernels for 13% -> 10%
where the time goes in v3:
time: 27.7 us; the launch traced here: 27.6 us
  Pallas kernels  11.2 us (40%)
  waiting for transfers between devices  9.87 us (36%)
  starting transfers between devices  6.46 us (23%)
    ppermute x4, waiting for transfers between devices, shifted(): return lax.ppermute(x, axis, [((i + by) % size, i) for i in range(size)])  9.87 us
    ppermute x4, starting transfers between devices, shifted(): return lax.ppermute(x, axis, [((i + by) % size, i) for i in range(size)])  6.46 us
    pallas_call x1, Pallas kernels, call_first(): pl.pallas_call(first_kernel, out_shape=[jax.ShapeDtypeStruct((256, 256),...  5.16 us
    pallas_call x1, Pallas kernels, call_second(): pl.pallas_call(second_kernel, out_shape=jax.ShapeDtypeStruct((16, 16, 256...  3.18 us
    pallas_call x1, Pallas kernels, call_bias(): pl.pallas_call(bias_kernel, out_shape=[jax.ShapeDtypeStruct((HEADS, 256,...  1.97 us
    pallas_call x1, Pallas kernels, call_early(): pl.pallas_call(early_kernel, out_shape=[jax.ShapeDtypeStruct((HEADS, 128,...  0.81 us
  transfers between devices with their start and end apart: 4, of which 2 were waited for; matrix products, arithmetic and copies ran while one was open for 0% of the time, Pallas kernels for 10%

profile of v3, /device:TPU:103, one launch (start us, length us, event | category | flops | bytes accessed | tf_op | source)
XLA Modules:
  0.0 27.6 jit_solution(14897013286907064582)
XLA Ops:
  0.0 5.2 %shard_map.100 = (f32[256,256]{1,0:T(8,128)S(1)}, f32[128,256]{1,0:T(8,128)S(1)}, f32[136,256]{1,0:T(8,128)S(1)}) custom-call(f32[16,16,256]{2,1,0:T(8,128)} %x_hbm.1, s32[256,256]{1,0:T(8,128)} %index.1, s32[16,16]{1,0:T(8,128)} %region_hbm.1, f32[2,8,961]{2,1,0:T(8,128)} %table.1, f32[2,2,256]{2,1,0:T(2,128)} %gain.1, f32[2,2,256]{2,1,0:T(2,128)} %shift.1, ...), custom_call_target="tpu_custom_call" | custom-call | flops 1000000000 | bytes 3145728 | tf_op jit(solution)/shard_map/pallas_call | solution.py:346
  5.2 1.3 %collective-permute-start = (f32[136,256]{1,0:T(8,128)S(1)}, f32[136,256]{1,0:T(8,128)S(1)}, u32[]{:S(2)}, u32[]{:S(2)}) collective-permute-start(f32[136,256]{1,0:T(8,128)S(1)} %get-tuple-element.17.bottom), channel_id=1, source_target_pairs={{224,0},{0,32},{32,64},{64,96},{96,128},{128,160},{160,192},{192,2... | collective-permute-start | bytes 417800 | tf_op jit(solution)/shard_map/ppermute | solution.py:334
  6.5 0.3 collective-permute-start.1
  6.7 0.0 copy-done.5
  6.7 0.0 copy-done.4
  6.7 2.0 %shard_map.101 = (f32[8,256,256]{2,1,0:T(8,128)S(1)}, f32[128,256]{1,0:T(8,128)S(1)}, f32[128,256]{1,0:T(8,128)S(1)}) custom-call(s32[256,256]{1,0:T(8,128)S(1)} %copy-done.4, f32[2,8,961]{2,1,0:T(8,128)S(1)} %copy-done.5, f32[128,256]{1,0:T(8,128)S(1)} %get-tuple-element.18.top, f32[136,256]{1,0:T(8,128)S(1)} %get-tuple-element.17.bottom), custom_call_target="tpu_custom_call" | custom-call | flops 1000000000 | bytes 8388608 | tf_op jit(solution)/shard_map/pallas_call | solution.py:378
  8.7 0.0 copy-start.2
  8.7 3.7 %collective-permute-done.1.south = f32[128,256]{1,0:T(8,128)S(1)} collective-permute-done((f32[128,256]{1,0:T(8,128)S(1)}, f32[128,256]{1,0:T(8,128)S(1)}, u32[]{:S(2)}, u32[]{:S(2)}) %collective-permute-start.1) | collective-permute-done | bytes 131104 | tf_op jit(solution)/shard_map/ppermute | solution.py:334
  12.4 0.0 collective-permute-done.north
  12.4 0.0 copy-start
  12.4 0.0 copy-start.1
  12.5 0.0 copy-start.3
  12.5 0.0 copy-start.6
  12.5 0.0 copy-start.7
  12.5 4.9 %collective-permute-start.2 = (f32[264,256]{1,0:T(8,128)S(1)}, f32[264,256]{1,0:T(8,128)S(1)}, u32[]{:S(2)}, u32[]{:S(2)}) collective-permute-start(f32[264,256]{1,0:T(8,128)S(1)} %get-tuple-element.21), channel_id=1, source_target_pairs={{31,0},{0,1},{1,2},{2,3},{3,4},{4,5},{5,6},{6,7},{7,8},{8,9},{9,10... | collective-permute-start | bytes 811016 | tf_op jit(solution)/shard_map/ppermute | solution.py:334
  17.4 0.0 collective-permute-start.3
  17.4 0.0 copy-done.2
  17.4 0.8 %shard_map.103 = (f32[8,128,256]{2,1,0:T(8,128)S(1)}, bf16[8,2,64,128]{3,2,1,0:T(8,128)(2,1)S(1)}, bf16[256,256]{1,0:T(8,128)(2,1)S(1)}) custom-call(f32[128,256]{1,0:T(8,128)S(1)} %get-tuple-element.18.top, f32[136,256]{1,0:T(8,128)S(1)} %get-tuple-element.17.bottom, f32[136,256]{1,0:T(8,128)S(1)} %collective-permute-done.north, ...), custom_call_target="tpu_custom_call" | custom-call | flops 1000000000 | bytes 8388608 | tf_op jit(solution)/shard_map/pallas_call | solution.py:408
  18.2 6.2 %collective-permute-done.3.east = f32[256,256]{1,0:T(8,128)S(1)} collective-permute-done((f32[256,256]{1,0:T(8,128)S(1)}, f32[256,256]{1,0:T(8,128)S(1)}, u32[]{:S(2)}, u32[]{:S(2)}) %collective-permute-start.3) | collective-permute-done | bytes 262176 | tf_op jit(solution)/shard_map/ppermute | solution.py:334
  24.4 0.0 collective-permute-done.2.west
  24.4 0.0 copy-done
  24.4 0.0 copy-done.1
  24.4 0.0 copy-done.3
  24.5 3.2 %shard_map.104 = f32[16,16,256]{2,1,0:T(8,128)} custom-call(f32[256,256]{1,0:T(8,128)S(1)} %get-tuple-element.16.x, f32[136,256]{1,0:T(8,128)S(1)} %get-tuple-element.17.bottom, f32[136,256]{1,0:T(8,128)S(1)} %collective-permute-done.north, f32[264,256]{1,0:T(8,128)S(1)} %collective-permute-done.2.west, f32[256,256]{1,0:T(8,128)S(1)} %collective-permute-done.3.east, ...), custom_call_target="tpu_custom_call" | custom-call | flops 1000000000 | bytes 3145728 | tf_op jit(solution)/shard_map/pallas_call | solution.py:427
  (5 shorter events, 0.0 us)
Async XLA Ops:
  0.0 6.7 %copy-start.5 = (f32[2,8,961]{2,1,0:T(8,128)S(1)}, f32[2,8,961]{2,1,0:T(8,128)}, u32[]{:S(2)}) copy-start(f32[2,8,961]{2,1,0:T(8,128)} %table.1) | copy-start | bytes 184516
  0.0 6.7 %copy-start.4 = (s32[256,256]{1,0:T(8,128)S(1)}, s32[256,256]{1,0:T(8,128)}, u32[]{:S(2)}) copy-start(s32[256,256]{1,0:T(8,128)} %index.1) | copy-start | bytes 786436
  5.2 7.2 %collective-permute-start = (f32[136,256]{1,0:T(8,128)S(1)}, f32[136,256]{1,0:T(8,128)S(1)}, u32[]{:S(2)}, u32[]{:S(2)}) collective-permute-start(f32[136,256]{1,0:T(8,128)S(1)} %get-tuple-element.17.bottom), channel_id=1, source_target_pairs={{224,0},{0,32},{32,64},{64,96},{96,128},{128,160},{160,192},{192,2... | collective-permute-start | bytes 417800 | tf_op jit(solution)/shard_map/ppermute | solution.py:334
  6.5 5.9 %collective-permute-start.1 = (f32[128,256]{1,0:T(8,128)S(1)}, f32[128,256]{1,0:T(8,128)S(1)}, u32[]{:S(2)}, u32[]{:S(2)}) collective-permute-start(f32[128,256]{1,0:T(8,128)S(1)} %get-tuple-element.18.top), channel_id=1, source_target_pairs={{32,0},{64,32},{96,64},{128,96},{160,128},{192,160},{224,192},{0,2... | collective-permute-start | bytes 393224 | tf_op jit(solution)/shard_map/ppermute | solution.py:334
  8.7 8.7 %copy-start.2 = (bf16[2,256,768]{2,1,0:T(8,128)(2,1)S(1)}, bf16[2,256,768]{2,1,0:T(8,128)(2,1)}, u32[]{:S(2)}) copy-start(bf16[2,256,768]{2,1,0:T(8,128)(2,1)} %wqkv.3) | copy-start | bytes 2359300
  12.4 12.0 %copy-start = (bf16[2,256,1024]{2,1,0:T(8,128)(2,1)S(1)}, bf16[2,256,1024]{2,1,0:T(8,128)(2,1)}, u32[]{:S(2)}) copy-start(bf16[2,256,1024]{2,1,0:T(8,128)(2,1)} %wexpand.1) | copy-start | bytes 3145732
  12.4 12.0 %copy-start.1 = (bf16[2,1024,256]{2,1,0:T(8,128)(2,1)S(1)}, bf16[2,1024,256]{2,1,0:T(8,128)(2,1)}, u32[]{:S(2)}) copy-start(bf16[2,1024,256]{2,1,0:T(8,128)(2,1)} %wreduce.1) | copy-start | bytes 3145732
  12.5 12.0 %copy-start.3 = (bf16[2,256,256]{2,1,0:T(8,128)(2,1)S(1)}, bf16[2,256,256]{2,1,0:T(8,128)(2,1)}, u32[]{:S(2)}) copy-start(bf16[2,256,256]{2,1,0:T(8,128)(2,1)} %wproj.1) | copy-start | bytes 786436
  12.5 12.0 %copy-start.6 = (f32[2,2,256]{2,1,0:T(2,128)S(1)}, f32[2,2,256]{2,1,0:T(2,128)}, u32[]{:S(2)}) copy-start(f32[2,2,256]{2,1,0:T(2,128)} %gain.1) | copy-start | bytes 12292
  12.5 12.0 %copy-start.7 = (f32[2,2,256]{2,1,0:T(2,128)S(1)}, f32[2,2,256]{2,1,0:T(2,128)}, u32[]{:S(2)}) copy-start(f32[2,2,256]{2,1,0:T(2,128)} %shift.1) | copy-start | bytes 12292
  12.5 11.9 %collective-permute-start.2 = (f32[264,256]{1,0:T(8,128)S(1)}, f32[264,256]{1,0:T(8,128)S(1)}, u32[]{:S(2)}, u32[]{:S(2)}) collective-permute-start(f32[264,256]{1,0:T(8,128)S(1)} %get-tuple-element.21), channel_id=1, source_target_pairs={{31,0},{0,1},{1,2},{2,3},{3,4},{4,5},{5,6},{6,7},{7,8},{8,9},{9,10... | collective-permute-start | bytes 811016 | tf_op jit(solution)/shard_map/ppermute | solution.py:334
  17.4 7.0 %collective-permute-start.3 = (f32[256,256]{1,0:T(8,128)S(1)}, f32[256,256]{1,0:T(8,128)S(1)}, u32[]{:S(2)}, u32[]{:S(2)}) collective-permute-start(f32[256,256]{1,0:T(8,128)S(1)} %get-tuple-element.22), channel_id=1, source_target_pairs={{1,0},{2,1},{3,2},{4,3},{5,4},{6,5},{7,6},{8,7},{9,8},{10,9},{11,1... | collective-permute-start | bytes 786440 | tf_op jit(solution)/shard_map/ppermute | solution.py:334

commit v4 on v3

--- a/solution.py
+++ b/solution.py
@@ -76,23 +76,24 @@
 
 
 AHEAD = 2
+LATE_AHEAD = 3
 EARLY = 64
-EACH = 11
-
-
-def attend(items, score, finish, beside=lambda step: None):
+EACH = 6
+
+
+def attend(items, score, finish, beside=lambda step: None, ahead=AHEAD):
     items = list(items)
     scores, raw = {}, {}
-    for i in range(len(items) + AHEAD + 1):
+    for i in range(len(items) + ahead + 1):
         if i < len(items):
             scores[i] = score(items[i])
         beside(2 * i)
-        if 0 <= i - AHEAD < len(items):
-            now = scores.pop(i - AHEAD)
-            raw[i - AHEAD] = jnp.exp2(now - jnp.max(now, 0, keepdims=True)).astype(BF16)
+        if 0 <= i - ahead < len(items):
+            now = scores.pop(i - ahead)
+            raw[i - ahead] = jnp.exp2(now - jnp.max(now, 0, keepdims=True)).astype(BF16)
         beside(2 * i + 1)
-        if i - AHEAD >= 1:
-            finish(items[i - AHEAD - 1], raw.pop(i - AHEAD - 1))
+        if i - ahead >= 1:
+            finish(items[i - ahead - 1], raw.pop(i - ahead - 1))
 
 
 def attention(x, normed, bias_ref, wqkv, wproj, joined_ref, beside):
@@ -178,7 +179,7 @@
         for words, tile in tiles:
             look_up_tile(lookup, index_t, bias, words, tile // 2 * 8, tile % 2)
 
-    tiles = [(words, tile) for words in ((0,), (1, 2)) for tile in range(64)]
+    tiles = [(words, tile) for words in ((0, 1), (2,)) for tile in range(64)]
     look_up(tiles[:EARLY])
     for copy in copies[2:8]:
         copy.wait()
@@ -242,16 +243,24 @@
             values[h, window // 2, window % 2 * 32 : window % 2 * 32 + 32, :] = value[h * 32 : h * 32 + 32]
 
 
-def cell_scores(keys, query, h, half):
+def cell_scores(keys, query, pair, half):
     row = lax.broadcasted_iota(jnp.int32, (128, 256), 0)
     lane = lax.broadcasted_iota(jnp.int32, (128, 256), 1)
-    pick = jnp.where((row // 64 == lane // 128) & (lane % 128 // 32 == h % 4), 1.0, 0.0).astype(BF16)
-    group = h // 4
+    group = pair // 2
     part = query[half * 128 : half * 128 + 128, group * 128 : group * 128 + 128]
+    part = jnp.concatenate([part, part], 1)
+    picks = [
+        jnp.where((row // 64 == lane // 128) & (lane % 128 // 32 == h % 4), 1.0, 0.0).astype(BF16)
+        for h in (2 * pair, 2 * pair + 1)
+    ]
     return lax.dot_general(
-        keys[group, half], jnp.concatenate([part, part], 1) * pick, (((1,), (1,)), ((), ())),
+        keys[group, half], jnp.concatenate([part * pick for pick in picks], 0), (((1,), (1,)), ((), ())),
         preferred_element_type=F32,
     )
+
+
+def both(ref, pair, rows, lanes):
+    return jnp.concatenate([ref[2 * pair, rows, lanes], ref[2 * pair + 1, rows, lanes]], 1)
 
 
 def early_kernel(top, bottom, north, south, bias, wqkv, scores, values, query, around, keys):
@@ -264,10 +273,12 @@
     own = jnp.concatenate([around[t, (1 - t // 2) * 64 : (2 - t // 2) * 64, :] for t in range(4)], 0)
     scaled = jnp.dot(own, wqkv[:, 0:256], preferred_element_type=F32)
     query[...] = (scaled * (LOG2E / math.sqrt(32.0))).astype(BF16)
-    for h in range(HEADS):
+    for pair in range(HEADS // 2):
         for half in range(2):
             lanes = slice(half * 128, half * 128 + 128)
-            scores[h, :, lanes] = cell_scores(keys, query, h, half) + bias[h, 0:128, lanes]
+            found = cell_scores(keys, query, pair, half) + both(bias, pair, slice(0, 128), lanes)
+            scores[2 * pair, :, lanes] = found[:, 0:128]
+            scores[2 * pair + 1, :, lanes] = found[:, 128:256]
 
 
 def second_kernel(
@@ -303,25 +314,30 @@
     ones = jnp.ones((16, 256), BF16)
 
     def score(item):
-        h, half = item
+        pair, half = item
         lanes = slice(half * 128, half * 128 + 128)
-        late = cell_scores(keys, query, h, half) + bias[h, 128:256, lanes]
-        return jnp.concatenate([early_scores[h, :, lanes], late], 0) + mask[:, lanes]
+        late = cell_scores(keys, query, pair, half) + both(bias, pair, slice(128, 256), lanes)
+        found = jnp.concatenate([both(early_scores, pair, slice(0, 128), lanes), late], 0)
+        return found + jnp.concatenate([mask[:, lanes]] * 2, 1)
 
     def finish(item, raw):
-        h, half = item
+        pair, half = item
         lanes = slice(half * 128, half * 128 + 128)
-        left = jnp.concatenate([jnp.concatenate([early_values[h, half], values[h, half]], 1), ones], 0)
-        sums = jnp.dot(left, raw, preferred_element_type=F32)
-        inverse = 1.0 / sums[64:72]
-        for j in range(2):
+        heads = (2 * pair, 2 * pair + 1)
+        left = [jnp.concatenate([early_values[h, half], values[h, half]], 1) for h in heads]
+        sums = jnp.dot(jnp.concatenate(left + [ones], 0), raw, preferred_element_type=F32)
+        for at, h in enumerate(heads):
+            mine = sums[:, at * 128 : at * 128 + 128]
+            inverse = 1.0 / mine[128:136]
             rows = [
-                jnp.where(left_cell, sums[at : at + 8], sums[at + 32 : at + 40]) * inverse
-                for at in (16 * j, 16 * j + 8)
+                jnp.where(left_cell, mine[i : i + 8], mine[i + 32 : i + 40]) * inverse
+                for i in range(at * 64, at * 64 + 32, 8)
             ]
-            joined[32 * h + 16 * j : 32 * h + 16 * j + 16, lanes] = jnp.concatenate(rows, 0).astype(BF16)
-
-    attend([(h, half) for h in range(HEADS) for half in range(2)], score, finish)
+            for j in range(2):
+                part = jnp.concatenate(rows[2 * j : 2 * j + 2], 0).astype(BF16)
+                joined[32 * h + 16 * j : 32 * h + 16 * j + 16, lanes] = part
+
+    attend([(pair, half) for pair in range(HEADS // 2) for half in range(2)], score, finish, ahead=LATE_AHEAD)
     attended = cell_order(x[...]) + lax.dot_general(
         joined[...], wproj[1], (((0,), (0,)), ((), ())), preferred_element_type=F32
     )

time: 27.7 us -> 27.4 us (0.989)
  Pallas kernels: 11.2 us -> 10.8 us
where the time goes in v4:
time: 27.4 us; the launch traced here: 27.3 us
  Pallas kernels  10.8 us (39%)
  waiting for transfers between devices  9.88 us (36%)
  starting transfers between devices  6.46 us (24%)
    ppermute x4, waiting for transfers between devices, shifted(): return lax.ppermute(x, axis, [((i + by) % size, i) for i in range(size)])  9.88 us
    ppermute x4, starting transfers between devices, shifted(): return lax.ppermute(x, axis, [((i + by) % size, i) for i in range(size)])  6.46 us
    pallas_call x1, Pallas kernels, call_first(): pl.pallas_call(first_kernel, out_shape=[jax.ShapeDtypeStruct((256, 256),...  5.08 us
    pallas_call x1, Pallas kernels, call_second(): pl.pallas_call(second_kernel, out_shape=jax.ShapeDtypeStruct((16, 16, 256...  2.92 us
    pallas_call x1, Pallas kernels, call_bias(): pl.pallas_call(bias_kernel, out_shape=[jax.ShapeDtypeStruct((HEADS, 256,...  1.97 us
    pallas_call x1, Pallas kernels, call_early(): pl.pallas_call(early_kernel, out_shape=[jax.ShapeDtypeStruct((HEADS, 128,...  0.8 us
  transfers between devices with their start and end apart: 4, of which 2 were waited for; matrix products, arithmetic and copies ran while one was open for 0% of the time, Pallas kernels for 10%

profile of v4, /device:TPU:103, one launch (start us, length us, event | category | flops | bytes accessed | tf_op | source)
XLA Modules:
  0.0 27.3 jit_solution(11712041337394066424)
XLA Ops:
  0.0 5.1 %shard_map.100 = (f32[256,256]{1,0:T(8,128)S(1)}, f32[128,256]{1,0:T(8,128)S(1)}, f32[136,256]{1,0:T(8,128)S(1)}) custom-call(f32[16,16,256]{2,1,0:T(8,128)} %x_hbm.1, s32[256,256]{1,0:T(8,128)} %index.1, s32[16,16]{1,0:T(8,128)} %region_hbm.1, f32[2,8,961]{2,1,0:T(8,128)} %table.1, f32[2,2,256]{2,1,0:T(2,128)} %gain.1, f32[2,2,256]{2,1,0:T(2,128)} %shift.1, ...), custom_call_target="tpu_custom_call" | custom-call | flops 1000000000 | bytes 3145728 | tf_op jit(solution)/shard_map/pallas_call | solution.py:362
  5.1 1.3 %collective-permute-start = (f32[136,256]{1,0:T(8,128)S(1)}, f32[136,256]{1,0:T(8,128)S(1)}, u32[]{:S(2)}, u32[]{:S(2)}) collective-permute-start(f32[136,256]{1,0:T(8,128)S(1)} %get-tuple-element.17.bottom), channel_id=1, source_target_pairs={{224,0},{0,32},{32,64},{64,96},{96,128},{128,160},{160,192},{192,2... | collective-permute-start | bytes 417800 | tf_op jit(solution)/shard_map/ppermute | solution.py:350
  6.4 0.3 collective-permute-start.1
  6.6 0.0 copy-done.5
  6.6 0.0 copy-done.4
  6.6 2.0 %shard_map.101 = (f32[8,256,256]{2,1,0:T(8,128)S(1)}, f32[128,256]{1,0:T(8,128)S(1)}, f32[128,256]{1,0:T(8,128)S(1)}) custom-call(s32[256,256]{1,0:T(8,128)S(1)} %copy-done.4, f32[2,8,961]{2,1,0:T(8,128)S(1)} %copy-done.5, f32[128,256]{1,0:T(8,128)S(1)} %get-tuple-element.18.top, f32[136,256]{1,0:T(8,128)S(1)} %get-tuple-element.17.bottom), custom_call_target="tpu_custom_call" | custom-call | flops 1000000000 | bytes 8388608 | tf_op jit(solution)/shard_map/pallas_call | solution.py:394
  8.6 0.0 copy-start.2
  8.6 3.7 %collective-permute-done.1.south = f32[128,256]{1,0:T(8,128)S(1)} collective-permute-done((f32[128,256]{1,0:T(8,128)S(1)}, f32[128,256]{1,0:T(8,128)S(1)}, u32[]{:S(2)}, u32[]{:S(2)}) %collective-permute-start.1) | collective-permute-done | bytes 131104 | tf_op jit(solution)/shard_map/ppermute | solution.py:350
  12.3 0.0 collective-permute-done.north
  12.4 0.0 copy-start
  12.4 0.0 copy-start.1
  12.4 0.0 copy-start.3
  12.4 0.0 copy-start.6
  12.4 0.0 copy-start.7
  12.4 4.9 %collective-permute-start.2 = (f32[264,256]{1,0:T(8,128)S(1)}, f32[264,256]{1,0:T(8,128)S(1)}, u32[]{:S(2)}, u32[]{:S(2)}) collective-permute-start(f32[264,256]{1,0:T(8,128)S(1)} %get-tuple-element.21), channel_id=1, source_target_pairs={{31,0},{0,1},{1,2},{2,3},{3,4},{4,5},{5,6},{6,7},{7,8},{8,9},{9,10... | collective-permute-start | bytes 811016 | tf_op jit(solution)/shard_map/ppermute | solution.py:350
  17.3 0.0 collective-permute-start.3
  17.3 0.0 copy-done.2
  17.3 0.8 %shard_map.103 = (f32[8,128,256]{2,1,0:T(8,128)S(1)}, bf16[8,2,64,128]{3,2,1,0:T(8,128)(2,1)S(1)}, bf16[256,256]{1,0:T(8,128)(2,1)S(1)}) custom-call(f32[128,256]{1,0:T(8,128)S(1)} %get-tuple-element.18.top, f32[136,256]{1,0:T(8,128)S(1)} %get-tuple-element.17.bottom, f32[136,256]{1,0:T(8,128)S(1)} %collective-permute-done.north, ...), custom_call_target="tpu_custom_call" | custom-call | flops 1000000000 | bytes 8388608 | tf_op jit(solution)/shard_map/pallas_call | solution.py:424
  18.1 6.2 %collective-permute-done.3.east = f32[256,256]{1,0:T(8,128)S(1)} collective-permute-done((f32[256,256]{1,0:T(8,128)S(1)}, f32[256,256]{1,0:T(8,128)S(1)}, u32[]{:S(2)}, u32[]{:S(2)}) %collective-permute-start.3) | collective-permute-done | bytes 262176 | tf_op jit(solution)/shard_map/ppermute | solution.py:350
  24.3 0.0 collective-permute-done.2.west
  24.3 0.0 copy-done
  24.4 0.0 copy-done.1
  24.4 0.0 copy-done.3
  24.4 2.9 %shard_map.104 = f32[16,16,256]{2,1,0:T(8,128)} custom-call(f32[256,256]{1,0:T(8,128)S(1)} %get-tuple-element.16.x, f32[136,256]{1,0:T(8,128)S(1)} %get-tuple-element.17.bottom, f32[136,256]{1,0:T(8,128)S(1)} %collective-permute-done.north, f32[264,256]{1,0:T(8,128)S(1)} %collective-permute-done.2.west, f32[256,256]{1,0:T(8,128)S(1)} %collective-permute-done.3.east, ...), custom_call_target="tpu_custom_call" | custom-call | flops 1000000000 | bytes 3145728 | tf_op jit(solution)/shard_map/pallas_call | solution.py:443
  (5 shorter events, 0.0 us)
Async XLA Ops:
  0.0 6.6 %copy-start.5 = (f32[2,8,961]{2,1,0:T(8,128)S(1)}, f32[2,8,961]{2,1,0:T(8,128)}, u32[]{:S(2)}) copy-start(f32[2,8,961]{2,1,0:T(8,128)} %table.1) | copy-start | bytes 184516
  0.0 6.6 %copy-start.4 = (s32[256,256]{1,0:T(8,128)S(1)}, s32[256,256]{1,0:T(8,128)}, u32[]{:S(2)}) copy-start(s32[256,256]{1,0:T(8,128)} %index.1) | copy-start | bytes 786436
  5.1 7.2 %collective-permute-start = (f32[136,256]{1,0:T(8,128)S(1)}, f32[136,256]{1,0:T(8,128)S(1)}, u32[]{:S(2)}, u32[]{:S(2)}) collective-permute-start(f32[136,256]{1,0:T(8,128)S(1)} %get-tuple-element.17.bottom), channel_id=1, source_target_pairs={{224,0},{0,32},{32,64},{64,96},{96,128},{128,160},{160,192},{192,2... | collective-permute-start | bytes 417800 | tf_op jit(solution)/shard_map/ppermute | solution.py:350
  6.4 5.9 %collective-permute-start.1 = (f32[128,256]{1,0:T(8,128)S(1)}, f32[128,256]{1,0:T(8,128)S(1)}, u32[]{:S(2)}, u32[]{:S(2)}) collective-permute-start(f32[128,256]{1,0:T(8,128)S(1)} %get-tuple-element.18.top), channel_id=1, source_target_pairs={{32,0},{64,32},{96,64},{128,96},{160,128},{192,160},{224,192},{0,2... | collective-permute-start | bytes 393224 | tf_op jit(solution)/shard_map/ppermute | solution.py:350
  8.6 8.7 %copy-start.2 = (bf16[2,256,768]{2,1,0:T(8,128)(2,1)S(1)}, bf16[2,256,768]{2,1,0:T(8,128)(2,1)}, u32[]{:S(2)}) copy-start(bf16[2,256,768]{2,1,0:T(8,128)(2,1)} %wqkv.3) | copy-start | bytes 2359300
  12.4 12.0 %copy-start = (bf16[2,256,1024]{2,1,0:T(8,128)(2,1)S(1)}, bf16[2,256,1024]{2,1,0:T(8,128)(2,1)}, u32[]{:S(2)}) copy-start(bf16[2,256,1024]{2,1,0:T(8,128)(2,1)} %wexpand.1) | copy-start | bytes 3145732
  12.4 12.0 %copy-start.1 = (bf16[2,1024,256]{2,1,0:T(8,128)(2,1)S(1)}, bf16[2,1024,256]{2,1,0:T(8,128)(2,1)}, u32[]{:S(2)}) copy-start(bf16[2,1024,256]{2,1,0:T(8,128)(2,1)} %wreduce.1) | copy-start | bytes 3145732
  12.4 12.0 %copy-start.3 = (bf16[2,256,256]{2,1,0:T(8,128)(2,1)S(1)}, bf16[2,256,256]{2,1,0:T(8,128)(2,1)}, u32[]{:S(2)}) copy-start(bf16[2,256,256]{2,1,0:T(8,128)(2,1)} %wproj.1) | copy-start | bytes 786436
  12.4 12.0 %copy-start.6 = (f32[2,2,256]{2,1,0:T(2,128)S(1)}, f32[2,2,256]{2,1,0:T(2,128)}, u32[]{:S(2)}) copy-start(f32[2,2,256]{2,1,0:T(2,128)} %gain.1) | copy-start | bytes 12292
  12.4 12.0 %copy-start.7 = (f32[2,2,256]{2,1,0:T(2,128)S(1)}, f32[2,2,256]{2,1,0:T(2,128)}, u32[]{:S(2)}) copy-start(f32[2,2,256]{2,1,0:T(2,128)} %shift.1) | copy-start | bytes 12292
  12.4 11.9 %collective-permute-start.2 = (f32[264,256]{1,0:T(8,128)S(1)}, f32[264,256]{1,0:T(8,128)S(1)}, u32[]{:S(2)}, u32[]{:S(2)}) collective-permute-start(f32[264,256]{1,0:T(8,128)S(1)} %get-tuple-element.21), channel_id=1, source_target_pairs={{31,0},{0,1},{1,2},{2,3},{3,4},{4,5},{5,6},{6,7},{7,8},{8,9},{9,10... | collective-permute-start | bytes 811016 | tf_op jit(solution)/shard_map/ppermute | solution.py:350
  17.3 7.0 %collective-permute-start.3 = (f32[256,256]{1,0:T(8,128)S(1)}, f32[256,256]{1,0:T(8,128)S(1)}, u32[]{:S(2)}, u32[]{:S(2)}) collective-permute-start(f32[256,256]{1,0:T(8,128)S(1)} %get-tuple-element.22), channel_id=1, source_target_pairs={{1,0},{2,1},{3,2},{4,3},{5,4},{6,5},{7,6},{8,7},{9,8},{10,9},{11,1... | collective-permute-start | bytes 786440 | tf_op jit(solution)/shard_map/ppermute | solution.py:350

commit v5 on v4

--- a/solution.py
+++ b/solution.py
@@ -134,16 +134,14 @@
         part = slice(j * 256, j * 256 + 256)
         hidden = jnp.dot(normed, wexpand[:, part], preferred_element_type=F32)
         hidden = (hidden * (0.5 * lax.erf(hidden * math.sqrt(0.5)) + 0.5)).astype(BF16)
-        total = total + jnp.dot(hidden, wreduce[part, :], preferred_element_type=F32)
-    return total
+        if j < 3:
+            total = total + jnp.dot(hidden, wreduce[part, :], preferred_element_type=F32)
+    for rows in (slice(0, 128), slice(128, 256)):
+        yield total[rows] + jnp.dot(hidden[rows], wreduce[part, :], preferred_element_type=F32)
 
 
 def cell_order(x):
     return jnp.swapaxes(x.reshape(2, 8, 2, 8, x.shape[-1]), 1, 2).reshape(x.shape)
-
-
-def from_cell_order(x):
-    return jnp.swapaxes(x.reshape(2, 2, 8, 8, x.shape[-1]), 1, 2).reshape(x.shape)
 
 
 def label_row(region):
@@ -193,7 +191,7 @@
     copies[8].wait()
     copies[9].wait()
     normed = layer_norm(attended, gain[0, 1:2], shift[0, 1:2])
-    total = feed_forward(attended, normed, wexpand, wreduce)
+    total = jnp.concatenate(list(feed_forward(attended, normed, wexpand, wreduce)), 0)
     out[...] = total
     normed = layer_norm(total, gain[1, 0:1], shift[1, 0:1]).astype(F32)
     top[...] = normed[0:128]
@@ -284,7 +282,7 @@
 def second_kernel(
     x, bottom, north, west, east, bias, early_scores, early_values, query, gain, shift, wqkv, wproj, wexpand, wreduce,
     out,
-    around, keys, values, mask, joined,
+    around, keys, values, mask, joined, result, sems,
 ):
     for grid_row in range(4):
         for b, ref in enumerate((west, east)):
@@ -342,8 +340,14 @@
         joined[...], wproj[1], (((0,), (0,)), ((), ())), preferred_element_type=F32
     )
     normed = layer_norm(attended, gain[1, 1:2], shift[1, 1:2])
-    total = feed_forward(attended, normed, wexpand.at[1], wreduce.at[1])
-    out[...] = from_cell_order(total).reshape(16, 16, 256)
+    copies = []
+    for a, total in enumerate(feed_forward(attended, normed, wexpand.at[1], wreduce.at[1])):
+        tile_rows = pl.ds(8 * a, 8)
+        result[tile_rows] = jnp.swapaxes(total.reshape(2, 8, 8, 256), 0, 1).reshape(8, 16, 256)
+        copies.append(pltpu.make_async_copy(result.at[tile_rows], out.at[tile_rows], sems.at[a]))
+        copies[a].start()
+    for copy in copies:
+        copy.wait()
 
 
 def shifted(x, axis, size, by):
@@ -444,13 +448,15 @@
         second_kernel,
         out_shape=jax.ShapeDtypeStruct((16, 16, 256), F32),
         in_specs=[VMEM] * 15,
-        out_specs=VMEM,
+        out_specs=HBM,
         scratch_shapes=[
             pltpu.VMEM((4, 128, 256), BF16),
             pltpu.VMEM((2, 2, 128, 256), BF16),
             pltpu.VMEM((HEADS, 2, 64, 128), BF16),
             pltpu.VMEM((256, 256), F32),
             pltpu.VMEM((256, 256), BF16),
+            pltpu.VMEM((16, 16, 256), F32),
+            pltpu.SemaphoreType.DMA((2,)),
         ],
         compiler_params=pltpu.CompilerParams(vmem_limit_bytes=16 << 20),
         cost_estimate=cost(3),

time: 27.4 us -> 27.4 us (level)
  no operation moved by 1% of the time
where the time goes in v5:
time: 27.4 us; the launch traced here: 27.3 us
  Pallas kernels  10.8 us (39%)
  waiting for transfers between devices  9.88 us (36%)
  starting transfers between devices  6.46 us (24%)
    ppermute x4, waiting for transfers between devices, shifted(): return lax.ppermute(x, axis, [((i + by) % size, i) for i in range(size)])  9.88 us
    ppermute x4, starting transfers between devices, shifted(): return lax.ppermute(x, axis, [((i + by) % size, i) for i in range(size)])  6.46 us
    pallas_call x1, Pallas kernels, call_first(): pl.pallas_call(first_kernel, out_shape=[jax.ShapeDtypeStruct((256, 256),...  5.08 us
    pallas_call x1, Pallas kernels, call_second(): pl.pallas_call(second_kernel, out_shape=jax.ShapeDtypeStruct((16, 16, 256...  2.9 us
    pallas_call x1, Pallas kernels, call_bias(): pl.pallas_call(bias_kernel, out_shape=[jax.ShapeDtypeStruct((HEADS, 256,...  1.97 us
    pallas_call x1, Pallas kernels, call_early(): pl.pallas_call(early_kernel, out_shape=[jax.ShapeDtypeStruct((HEADS, 128,...  0.8 us
  transfers between devices with their start and end apart: 4, of which 2 were waited for; matrix products, arithmetic and copies ran while one was open for 0% of the time, Pallas kernels for 10%

profile of v5, /device:TPU:103, one launch (start us, length us, event | category | flops | bytes accessed | tf_op | source)
XLA Modules:
  0.0 27.3 jit_solution(2954580201581038040)
XLA Ops:
  0.0 5.1 %shard_map.100 = (f32[256,256]{1,0:T(8,128)S(1)}, f32[128,256]{1,0:T(8,128)S(1)}, f32[136,256]{1,0:T(8,128)S(1)}) custom-call(f32[16,16,256]{2,1,0:T(8,128)} %x_hbm.1, s32[256,256]{1,0:T(8,128)} %index.1, s32[16,16]{1,0:T(8,128)} %region_hbm.1, f32[2,8,961]{2,1,0:T(8,128)} %table.1, f32[2,2,256]{2,1,0:T(2,128)} %gain.1, f32[2,2,256]{2,1,0:T(2,128)} %shift.1, ...), custom_call_target="tpu_custom_call" | custom-call | flops 1000000000 | bytes 3145728 | tf_op jit(solution)/shard_map/pallas_call | solution.py:366
  5.1 1.3 %collective-permute-start = (f32[136,256]{1,0:T(8,128)S(1)}, f32[136,256]{1,0:T(8,128)S(1)}, u32[]{:S(2)}, u32[]{:S(2)}) collective-permute-start(f32[136,256]{1,0:T(8,128)S(1)} %get-tuple-element.17.bottom), channel_id=1, source_target_pairs={{224,0},{0,32},{32,64},{64,96},{96,128},{128,160},{160,192},{192,2... | collective-permute-start | bytes 417800 | tf_op jit(solution)/shard_map/ppermute | solution.py:354
  6.4 0.3 collective-permute-start.1
  6.6 0.0 copy-done.5
  6.6 0.0 copy-done.4
  6.6 2.0 %shard_map.101 = (f32[8,256,256]{2,1,0:T(8,128)S(1)}, f32[128,256]{1,0:T(8,128)S(1)}, f32[128,256]{1,0:T(8,128)S(1)}) custom-call(s32[256,256]{1,0:T(8,128)S(1)} %copy-done.4, f32[2,8,961]{2,1,0:T(8,128)S(1)} %copy-done.5, f32[128,256]{1,0:T(8,128)S(1)} %get-tuple-element.18.top, f32[136,256]{1,0:T(8,128)S(1)} %get-tuple-element.17.bottom), custom_call_target="tpu_custom_call" | custom-call | flops 1000000000 | bytes 8388608 | tf_op jit(solution)/shard_map/pallas_call | solution.py:398
  8.6 0.0 copy-start.2
  8.6 3.7 %collective-permute-done.1.south = f32[128,256]{1,0:T(8,128)S(1)} collective-permute-done((f32[128,256]{1,0:T(8,128)S(1)}, f32[128,256]{1,0:T(8,128)S(1)}, u32[]{:S(2)}, u32[]{:S(2)}) %collective-permute-start.1) | collective-permute-done | bytes 131104 | tf_op jit(solution)/shard_map/ppermute | solution.py:354
  12.3 0.0 collective-permute-done.north
  12.4 0.0 copy-start
  12.4 0.0 copy-start.1
  12.4 0.0 copy-start.3
  12.4 0.0 copy-start.6
  12.4 0.0 copy-start.7
  12.4 4.9 %collective-permute-start.2 = (f32[264,256]{1,0:T(8,128)S(1)}, f32[264,256]{1,0:T(8,128)S(1)}, u32[]{:S(2)}, u32[]{:S(2)}) collective-permute-start(f32[264,256]{1,0:T(8,128)S(1)} %get-tuple-element.21), channel_id=1, source_target_pairs={{31,0},{0,1},{1,2},{2,3},{3,4},{4,5},{5,6},{6,7},{7,8},{8,9},{9,10... | collective-permute-start | bytes 811016 | tf_op jit(solution)/shard_map/ppermute | solution.py:354
  17.3 0.0 collective-permute-start.3
  17.3 0.0 copy-done.2
  17.3 0.8 %shard_map.103 = (f32[8,128,256]{2,1,0:T(8,128)S(1)}, bf16[8,2,64,128]{3,2,1,0:T(8,128)(2,1)S(1)}, bf16[256,256]{1,0:T(8,128)(2,1)S(1)}) custom-call(f32[128,256]{1,0:T(8,128)S(1)} %get-tuple-element.18.top, f32[136,256]{1,0:T(8,128)S(1)} %get-tuple-element.17.bottom, f32[136,256]{1,0:T(8,128)S(1)} %collective-permute-done.north, ...), custom_call_target="tpu_custom_call" | custom-call | flops 1000000000 | bytes 8388608 | tf_op jit(solution)/shard_map/pallas_call | solution.py:428
  18.1 6.2 %collective-permute-done.3.east = f32[256,256]{1,0:T(8,128)S(1)} collective-permute-done((f32[256,256]{1,0:T(8,128)S(1)}, f32[256,256]{1,0:T(8,128)S(1)}, u32[]{:S(2)}, u32[]{:S(2)}) %collective-permute-start.3) | collective-permute-done | bytes 262176 | tf_op jit(solution)/shard_map/ppermute | solution.py:354
  24.3 0.0 collective-permute-done.2.west
  24.3 0.0 copy-done
  24.4 0.0 copy-done.1
  24.4 0.0 copy-done.3
  24.4 2.9 %shard_map.104 = f32[16,16,256]{2,1,0:T(8,128)} custom-call(f32[256,256]{1,0:T(8,128)S(1)} %get-tuple-element.16.x, f32[136,256]{1,0:T(8,128)S(1)} %get-tuple-element.17.bottom, f32[136,256]{1,0:T(8,128)S(1)} %collective-permute-done.north, f32[264,256]{1,0:T(8,128)S(1)} %collective-permute-done.2.west, f32[256,256]{1,0:T(8,128)S(1)} %collective-permute-done.3.east, ...), custom_call_target="tpu_custom_call" | custom-call | flops 1000000000 | bytes 3145728 | tf_op jit(solution)/shard_map/pallas_call | solution.py:447
  (5 shorter events, 0.0 us)
Async XLA Ops:
  0.0 6.6 %copy-start.5 = (f32[2,8,961]{2,1,0:T(8,128)S(1)}, f32[2,8,961]{2,1,0:T(8,128)}, u32[]{:S(2)}) copy-start(f32[2,8,961]{2,1,0:T(8,128)} %table.1) | copy-start | bytes 184516
  0.0 6.6 %copy-start.4 = (s32[256,256]{1,0:T(8,128)S(1)}, s32[256,256]{1,0:T(8,128)}, u32[]{:S(2)}) copy-start(s32[256,256]{1,0:T(8,128)} %index.1) | copy-start | bytes 786436
  5.1 7.2 %collective-permute-start = (f32[136,256]{1,0:T(8,128)S(1)}, f32[136,256]{1,0:T(8,128)S(1)}, u32[]{:S(2)}, u32[]{:S(2)}) collective-permute-start(f32[136,256]{1,0:T(8,128)S(1)} %get-tuple-element.17.bottom), channel_id=1, source_target_pairs={{224,0},{0,32},{32,64},{64,96},{96,128},{128,160},{160,192},{192,2... | collective-permute-start | bytes 417800 | tf_op jit(solution)/shard_map/ppermute | solution.py:354
  6.4 5.9 %collective-permute-start.1 = (f32[128,256]{1,0:T(8,128)S(1)}, f32[128,256]{1,0:T(8,128)S(1)}, u32[]{:S(2)}, u32[]{:S(2)}) collective-permute-start(f32[128,256]{1,0:T(8,128)S(1)} %get-tuple-element.18.top), channel_id=1, source_target_pairs={{32,0},{64,32},{96,64},{128,96},{160,128},{192,160},{224,192},{0,2... | collective-permute-start | bytes 393224 | tf_op jit(solution)/shard_map/ppermute | solution.py:354
  8.6 8.7 %copy-start.2 = (bf16[2,256,768]{2,1,0:T(8,128)(2,1)S(1)}, bf16[2,256,768]{2,1,0:T(8,128)(2,1)}, u32[]{:S(2)}) copy-start(bf16[2,256,768]{2,1,0:T(8,128)(2,1)} %wqkv.3) | copy-start | bytes 2359300
  12.4 12.0 %copy-start = (bf16[2,256,1024]{2,1,0:T(8,128)(2,1)S(1)}, bf16[2,256,1024]{2,1,0:T(8,128)(2,1)}, u32[]{:S(2)}) copy-start(bf16[2,256,1024]{2,1,0:T(8,128)(2,1)} %wexpand.1) | copy-start | bytes 3145732
  12.4 12.0 %copy-start.1 = (bf16[2,1024,256]{2,1,0:T(8,128)(2,1)S(1)}, bf16[2,1024,256]{2,1,0:T(8,128)(2,1)}, u32[]{:S(2)}) copy-start(bf16[2,1024,256]{2,1,0:T(8,128)(2,1)} %wreduce.1) | copy-start | bytes 3145732
  12.4 12.0 %copy-start.3 = (bf16[2,256,256]{2,1,0:T(8,128)(2,1)S(1)}, bf16[2,256,256]{2,1,0:T(8,128)(2,1)}, u32[]{:S(2)}) copy-start(bf16[2,256,256]{2,1,0:T(8,128)(2,1)} %wproj.1) | copy-start | bytes 786436
  12.4 12.0 %copy-start.6 = (f32[2,2,256]{2,1,0:T(2,128)S(1)}, f32[2,2,256]{2,1,0:T(2,128)}, u32[]{:S(2)}) copy-start(f32[2,2,256]{2,1,0:T(2,128)} %gain.1) | copy-start | bytes 12292
  12.4 12.0 %copy-start.7 = (f32[2,2,256]{2,1,0:T(2,128)S(1)}, f32[2,2,256]{2,1,0:T(2,128)}, u32[]{:S(2)}) copy-start(f32[2,2,256]{2,1,0:T(2,128)} %shift.1) | copy-start | bytes 12292
  12.4 11.9 %collective-permute-start.2 = (f32[264,256]{1,0:T(8,128)S(1)}, f32[264,256]{1,0:T(8,128)S(1)}, u32[]{:S(2)}, u32[]{:S(2)}) collective-permute-start(f32[264,256]{1,0:T(8,128)S(1)} %get-tuple-element.21), channel_id=1, source_target_pairs={{31,0},{0,1},{1,2},{2,3},{3,4},{4,5},{5,6},{6,7},{7,8},{8,9},{9,10... | collective-permute-start | bytes 811016 | tf_op jit(solution)/shard_map/ppermute | solution.py:354
  17.3 7.0 %collective-permute-start.3 = (f32[256,256]{1,0:T(8,128)S(1)}, f32[256,256]{1,0:T(8,128)S(1)}, u32[]{:S(2)}, u32[]{:S(2)}) collective-permute-start(f32[256,256]{1,0:T(8,128)S(1)} %get-tuple-element.22), channel_id=1, source_target_pairs={{1,0},{2,1},{3,2},{4,3},{5,4},{6,5},{7,6},{8,7},{9,8},{10,9},{11,1... | collective-permute-start | bytes 786440 | tf_op jit(solution)/shard_map/ppermute | solution.py:354

commit v6 on v4

--- a/solution.py
+++ b/solution.py
@@ -130,8 +130,8 @@
 
 def feed_forward(attended, normed, wexpand, wreduce):
     total = attended
-    for j in range(4):
-        part = slice(j * 256, j * 256 + 256)
+    for j in range(2):
+        part = slice(j * 512, j * 512 + 512)
         hidden = jnp.dot(normed, wexpand[:, part], preferred_element_type=F32)
         hidden = (hidden * (0.5 * lax.erf(hidden * math.sqrt(0.5)) + 0.5)).astype(BF16)
         total = total + jnp.dot(hidden, wreduce[part, :], preferred_element_type=F32)

time: 27.4 us -> 27.5 us (level)
  no operation moved by 1% of the time
where the time goes in v6:
time: 27.5 us; the launch traced here: 27.4 us
  Pallas kernels  10.9 us (40%)
  waiting for transfers between devices  9.87 us (36%)
  starting transfers between devices  6.47 us (24%)
    ppermute x4, waiting for transfers between devices, shifted(): return lax.ppermute(x, axis, [((i + by) % size, i) for i in range(size)])  9.87 us
    ppermute x4, starting transfers between devices, shifted(): return lax.ppermute(x, axis, [((i + by) % size, i) for i in range(size)])  6.47 us
    pallas_call x1, Pallas kernels, call_first(): pl.pallas_call(first_kernel, out_shape=[jax.ShapeDtypeStruct((256, 256),...  5.17 us
    pallas_call x1, Pallas kernels, call_second(): pl.pallas_call(second_kernel, out_shape=jax.ShapeDtypeStruct((16, 16, 256...  2.91 us
    pallas_call x1, Pallas kernels, call_bias(): pl.pallas_call(bias_kernel, out_shape=[jax.ShapeDtypeStruct((HEADS, 256,...  1.97 us
    pallas_call x1, Pallas kernels, call_early(): pl.pallas_call(early_kernel, out_shape=[jax.ShapeDtypeStruct((HEADS, 128,...  0.81 us
  transfers between devices with their start and end apart: 4, of which 2 were waited for; matrix products, arithmetic and copies ran while one was open for 0% of the time, Pallas kernels for 10%

profile of v6, /device:TPU:103, one launch (start us, length us, event | category | flops | bytes accessed | tf_op | source)
XLA Modules:
  0.0 27.4 jit_solution(13176387136181908360)
XLA Ops:
  0.0 5.2 %shard_map.100 = (f32[256,256]{1,0:T(8,128)S(1)}, f32[128,256]{1,0:T(8,128)S(1)}, f32[136,256]{1,0:T(8,128)S(1)}) custom-call(f32[16,16,256]{2,1,0:T(8,128)} %x_hbm.1, s32[256,256]{1,0:T(8,128)} %index.1, s32[16,16]{1,0:T(8,128)} %region_hbm.1, f32[2,8,961]{2,1,0:T(8,128)} %table.1, f32[2,2,256]{2,1,0:T(2,128)} %gain.1, f32[2,2,256]{2,1,0:T(2,128)} %shift.1, ...), custom_call_target="tpu_custom_call" | custom-call | flops 1000000000 | bytes 3145728 | tf_op jit(solution)/shard_map/pallas_call | solution.py:362
  5.2 1.3 %collective-permute-start = (f32[136,256]{1,0:T(8,128)S(1)}, f32[136,256]{1,0:T(8,128)S(1)}, u32[]{:S(2)}, u32[]{:S(2)}) collective-permute-start(f32[136,256]{1,0:T(8,128)S(1)} %get-tuple-element.17.bottom), channel_id=1, source_target_pairs={{224,0},{0,32},{32,64},{64,96},{96,128},{128,160},{160,192},{192,2... | collective-permute-start | bytes 417800 | tf_op jit(solution)/shard_map/ppermute | solution.py:350
  6.5 0.3 collective-permute-start.1
  6.7 0.0 copy-done.5
  6.7 0.0 copy-done.4
  6.7 2.0 %shard_map.101 = (f32[8,256,256]{2,1,0:T(8,128)S(1)}, f32[128,256]{1,0:T(8,128)S(1)}, f32[128,256]{1,0:T(8,128)S(1)}) custom-call(s32[256,256]{1,0:T(8,128)S(1)} %copy-done.4, f32[2,8,961]{2,1,0:T(8,128)S(1)} %copy-done.5, f32[128,256]{1,0:T(8,128)S(1)} %get-tuple-element.18.top, f32[136,256]{1,0:T(8,128)S(1)} %get-tuple-element.17.bottom), custom_call_target="tpu_custom_call" | custom-call | flops 1000000000 | bytes 8388608 | tf_op jit(solution)/shard_map/pallas_call | solution.py:394
  8.7 0.0 copy-start.2
  8.7 3.7 %collective-permute-done.1.south = f32[128,256]{1,0:T(8,128)S(1)} collective-permute-done((f32[128,256]{1,0:T(8,128)S(1)}, f32[128,256]{1,0:T(8,128)S(1)}, u32[]{:S(2)}, u32[]{:S(2)}) %collective-permute-start.1) | collective-permute-done | bytes 131104 | tf_op jit(solution)/shard_map/ppermute | solution.py:350
  12.4 0.0 collective-permute-done.north
  12.4 0.0 copy-start
  12.5 0.0 copy-start.1
  12.5 0.0 copy-start.3
  12.5 0.0 copy-start.6
  12.5 0.0 copy-start.7
  12.5 4.9 %collective-permute-start.2 = (f32[264,256]{1,0:T(8,128)S(1)}, f32[264,256]{1,0:T(8,128)S(1)}, u32[]{:S(2)}, u32[]{:S(2)}) collective-permute-start(f32[264,256]{1,0:T(8,128)S(1)} %get-tuple-element.21), channel_id=1, source_target_pairs={{31,0},{0,1},{1,2},{2,3},{3,4},{4,5},{5,6},{6,7},{7,8},{8,9},{9,10... | collective-permute-start | bytes 811016 | tf_op jit(solution)/shard_map/ppermute | solution.py:350
  17.4 0.0 collective-permute-start.3
  17.4 0.0 copy-done.2
  17.4 0.8 %shard_map.103 = (f32[8,128,256]{2,1,0:T(8,128)S(1)}, bf16[8,2,64,128]{3,2,1,0:T(8,128)(2,1)S(1)}, bf16[256,256]{1,0:T(8,128)(2,1)S(1)}) custom-call(f32[128,256]{1,0:T(8,128)S(1)} %get-tuple-element.18.top, f32[136,256]{1,0:T(8,128)S(1)} %get-tuple-element.17.bottom, f32[136,256]{1,0:T(8,128)S(1)} %collective-permute-done.north, ...), custom_call_target="tpu_custom_call" | custom-call | flops 1000000000 | bytes 8388608 | tf_op jit(solution)/shard_map/pallas_call | solution.py:424
  18.2 6.2 %collective-permute-done.3.east = f32[256,256]{1,0:T(8,128)S(1)} collective-permute-done((f32[256,256]{1,0:T(8,128)S(1)}, f32[256,256]{1,0:T(8,128)S(1)}, u32[]{:S(2)}, u32[]{:S(2)}) %collective-permute-start.3) | collective-permute-done | bytes 262176 | tf_op jit(solution)/shard_map/ppermute | solution.py:350
  24.4 0.0 collective-permute-done.2.west
  24.4 0.0 copy-done
  24.4 0.0 copy-done.1
  24.4 0.0 copy-done.3
  24.5 2.9 %shard_map.104 = f32[16,16,256]{2,1,0:T(8,128)} custom-call(f32[256,256]{1,0:T(8,128)S(1)} %get-tuple-element.16.x, f32[136,256]{1,0:T(8,128)S(1)} %get-tuple-element.17.bottom, f32[136,256]{1,0:T(8,128)S(1)} %collective-permute-done.north, f32[264,256]{1,0:T(8,128)S(1)} %collective-permute-done.2.west, f32[256,256]{1,0:T(8,128)S(1)} %collective-permute-done.3.east, ...), custom_call_target="tpu_custom_call" | custom-call | flops 1000000000 | bytes 3145728 | tf_op jit(solution)/shard_map/pallas_call | solution.py:443
  (5 shorter events, 0.0 us)
Async XLA Ops:
  0.0 6.7 %copy-start.5 = (f32[2,8,961]{2,1,0:T(8,128)S(1)}, f32[2,8,961]{2,1,0:T(8,128)}, u32[]{:S(2)}) copy-start(f32[2,8,961]{2,1,0:T(8,128)} %table.1) | copy-start | bytes 184516
  0.0 6.7 %copy-start.4 = (s32[256,256]{1,0:T(8,128)S(1)}, s32[256,256]{1,0:T(8,128)}, u32[]{:S(2)}) copy-start(s32[256,256]{1,0:T(8,128)} %index.1) | copy-start | bytes 786436
  5.2 7.2 %collective-permute-start = (f32[136,256]{1,0:T(8,128)S(1)}, f32[136,256]{1,0:T(8,128)S(1)}, u32[]{:S(2)}, u32[]{:S(2)}) collective-permute-start(f32[136,256]{1,0:T(8,128)S(1)} %get-tuple-element.17.bottom), channel_id=1, source_target_pairs={{224,0},{0,32},{32,64},{64,96},{96,128},{128,160},{160,192},{192,2... | collective-permute-start | bytes 417800 | tf_op jit(solution)/shard_map/ppermute | solution.py:350
  6.5 5.9 %collective-permute-start.1 = (f32[128,256]{1,0:T(8,128)S(1)}, f32[128,256]{1,0:T(8,128)S(1)}, u32[]{:S(2)}, u32[]{:S(2)}) collective-permute-start(f32[128,256]{1,0:T(8,128)S(1)} %get-tuple-element.18.top), channel_id=1, source_target_pairs={{32,0},{64,32},{96,64},{128,96},{160,128},{192,160},{224,192},{0,2... | collective-permute-start | bytes 393224 | tf_op jit(solution)/shard_map/ppermute | solution.py:350
  8.7 8.7 %copy-start.2 = (bf16[2,256,768]{2,1,0:T(8,128)(2,1)S(1)}, bf16[2,256,768]{2,1,0:T(8,128)(2,1)}, u32[]{:S(2)}) copy-start(bf16[2,256,768]{2,1,0:T(8,128)(2,1)} %wqkv.3) | copy-start | bytes 2359300
  12.4 12.0 %copy-start = (bf16[2,256,1024]{2,1,0:T(8,128)(2,1)S(1)}, bf16[2,256,1024]{2,1,0:T(8,128)(2,1)}, u32[]{:S(2)}) copy-start(bf16[2,256,1024]{2,1,0:T(8,128)(2,1)} %wexpand.1) | copy-start | bytes 3145732
  12.5 12.0 %copy-start.1 = (bf16[2,1024,256]{2,1,0:T(8,128)(2,1)S(1)}, bf16[2,1024,256]{2,1,0:T(8,128)(2,1)}, u32[]{:S(2)}) copy-start(bf16[2,1024,256]{2,1,0:T(8,128)(2,1)} %wreduce.1) | copy-start | bytes 3145732
  12.5 12.0 %copy-start.3 = (bf16[2,256,256]{2,1,0:T(8,128)(2,1)S(1)}, bf16[2,256,256]{2,1,0:T(8,128)(2,1)}, u32[]{:S(2)}) copy-start(bf16[2,256,256]{2,1,0:T(8,128)(2,1)} %wproj.1) | copy-start | bytes 786436
  12.5 12.0 %copy-start.6 = (f32[2,2,256]{2,1,0:T(2,128)S(1)}, f32[2,2,256]{2,1,0:T(2,128)}, u32[]{:S(2)}) copy-start(f32[2,2,256]{2,1,0:T(2,128)} %gain.1) | copy-start | bytes 12292
  12.5 12.0 %copy-start.7 = (f32[2,2,256]{2,1,0:T(2,128)S(1)}, f32[2,2,256]{2,1,0:T(2,128)}, u32[]{:S(2)}) copy-start(f32[2,2,256]{2,1,0:T(2,128)} %shift.1) | copy-start | bytes 12292
  12.5 11.9 %collective-permute-start.2 = (f32[264,256]{1,0:T(8,128)S(1)}, f32[264,256]{1,0:T(8,128)S(1)}, u32[]{:S(2)}, u32[]{:S(2)}) collective-permute-start(f32[264,256]{1,0:T(8,128)S(1)} %get-tuple-element.21), channel_id=1, source_target_pairs={{31,0},{0,1},{1,2},{2,3},{3,4},{4,5},{5,6},{6,7},{7,8},{8,9},{9,10... | collective-permute-start | bytes 811016 | tf_op jit(solution)/shard_map/ppermute | solution.py:350
  17.4 7.0 %collective-permute-start.3 = (f32[256,256]{1,0:T(8,128)S(1)}, f32[256,256]{1,0:T(8,128)S(1)}, u32[]{:S(2)}, u32[]{:S(2)}) collective-permute-start(f32[256,256]{1,0:T(8,128)S(1)} %get-tuple-element.22), channel_id=1, source_target_pairs={{1,0},{2,1},{3,2},{4,3},{5,4},{6,5},{7,6},{8,7},{9,8},{10,9},{11,1... | collective-permute-start | bytes 786440 | tf_op jit(solution)/shard_map/ppermute | solution.py:350
